TPU v7x, 32 devices: a whole 2x2x4 slice. The times are simulated.
32 devices in a mesh: clip: 2 (over x), tm: 2 (over core), space: 8 (over z, y).
Axes of the slice: x: 2, y: 2, z: 4, core: 2. Of those that a mesh axis runs over, the one named last changes fastest.
Arguments:
- queue_latents: float32 [16, 2, 16, 128], P(('clip', 'tm'), None, None, 'space'), parts along dimension 0, may hold values from -6 to 6
- fresh_noise: float32 [6, 2, 16, 128], P('clip', None, None, 'space'), parts along dimension 0, may hold values from -6 to 6
- slot_levels: int32 [16], P('clip'), parts along dimension 0, may hold values from 1 to 15, as said below
- level_table: float32 [16, 8, 1152], replicated, may hold values from -2.5 to 2.5
- embed_weight: float32 [16, 1152], replicated, may hold values from -1.5 to 1.5
- spatial_in: bfloat16 [1152, 1728], replicated, may hold values from -0.1875 to 0.1875
- spatial_out: bfloat16 [576, 1152], replicated, may hold values from -0.25 to 0.25
- temporal_in: bfloat16 [1152, 1728], replicated, may hold values from -0.1875 to 0.1875
- temporal_out: bfloat16 [576, 1152], replicated, may hold values from -0.25 to 0.25
- norm_gains: float32 [4, 72], replicated, may hold values from 0.1 to 1.9
- final_weight: float32 [1152, 16], replicated, may hold values from -0.1875 to 0.1875
Outputs:
- next_queue: float32 [16, 2, 16, 128], P(('clip', 'tm'), None, None, 'space'), parts along dimension 0
- denoised: float32 [16, 2, 16, 128], P(('clip', 'tm'), None, None, 'space'), parts along dimension 0
There are 2 independent parts, one for each index of `clip`. A program takes and returns all parts, laid end to end along the dimension named above; an argument that names none is the same for every part. Nothing has to cross between parts.
Inputs may be any that keep to these rules, and one draw needn't show every extreme that they name: `slot_levels`: strictly rising along the queue; neighbouring slots differ by 1 or 2; the last slot holds 15.
All inputs are finite; a program needn't handle non-finite values.
Results may differ from a plain program's by a relative error of at most 0.0023.
Values may be sent and summed in bfloat16 or wider, within the bound.
No kernel may reach another device: no remote copies, remote signals or barrier semaphores. Data moves between devices by JAX's collectives and lax.ppermute only.
A program may use at most 128 MiB of HBM per device.

v0:
```python
import functools
import math

import jax
import jax.numpy as jnp
import numpy as np
from jax import lax
from jax.experimental import pallas as pl
from jax.experimental.pallas import tpu as pltpu
from jax.sharding import PartitionSpec as P

D = 1152
HEADS = 8
HD = 72
INNER = HEADS * HD
CH = 16
FRAMES = 2
STEPS = 3
LEVELS = 16

LANES = 128
WIDE = -(-INNER // LANES) * LANES
PIECE = 32
PACK = LANES // PIECE
PLAN = LANES + PIECE

GRANT = 24 * 1024 * 1024

epsilon = 1e-06
f32 = jnp.float32
bf16 = jnp.bfloat16


def dot(a, b):
    return lax.dot_general(a, b, (((1,), (0,)), ((), ())), preferred_element_type=f32)


def dot_nt(a, b):
    return lax.dot_general(a, b, (((1,), (1,)), ((), ())), preferred_element_type=f32)


def split(x):
    high = x.astype(bf16)
    return high, (x - high.astype(f32)).astype(bf16)


def sincos(count, width):
    half = width // 2
    rates = np.exp(-np.log(10000.0) * np.arange(half) / half)
    angles = np.arange(count)[:, None] * rates[None, :]
    return np.concatenate([np.sin(angles), np.cos(angles)], axis=-1)


def head_masks():
    shape = (HEADS, 1, WIDE)
    head = lax.broadcasted_iota(jnp.int32, shape, 0)
    position = lax.broadcasted_iota(jnp.int32, shape, 2)
    return ((position >= head * HD) & (position < (head + 1) * HD)).astype(f32)


def normalized(values):
    centered = values - jnp.mean(values, axis=-1, keepdims=True)
    return centered * lax.rsqrt(jnp.mean(centered * centered, axis=-1, keepdims=True) + epsilon)


def modulated(values, shift, scale):
    slots = shift.shape[0]
    out = values.reshape(slots, -1, D) * (1.0 + scale)[:, None, :] + shift[:, None, :]
    return out.reshape(values.shape)


def own_hidden(lat, embed, pos_own):
    lanes = lat.shape[1]
    lat_high, lat_low = split(lat)
    lat_high = lat_high.astype(f32)
    zeros = jnp.zeros((LANES - 3 * CH, lanes), f32)
    rows = jnp.concatenate([lat_high, lat_low.astype(f32), lat_high, zeros], axis=0).T.astype(bf16)
    embed_high, embed_low = split(embed)
    weights = jnp.concatenate(
        [embed_high, embed_high, embed_low, jnp.zeros((LANES - 3 * CH, D), bf16)], axis=0
    )
    own = pos_own.shape[0]
    return (dot(rows, weights).reshape(lanes // own, own, D) + pos_own[None]).reshape(lanes, D)


def make_piece(lat, embed, pos_own):
    lanes = lat.shape[1]
    hidden = own_hidden(lat, embed, pos_own)
    centered = hidden - jnp.mean(hidden, axis=-1, keepdims=True)
    deviation = jnp.sqrt(jnp.mean(centered * centered, axis=-1, keepdims=True) + epsilon)
    row = jnp.broadcast_to(deviation, (lanes, LANES)).T[:1]
    high, low = split(row)
    high = high.astype(f32)
    zeros = jnp.zeros((PIECE - CH - 3, lanes), f32)
    return jnp.concatenate([lat, high, high, low.astype(f32), zeros], axis=0).astype(bf16)


def placed(block, start):
    rows, width = block.shape
    wide = jnp.concatenate([block, jnp.zeros((rows, LANES - width), f32)], axis=1)
    return pltpu.roll(wide, start, 1) if start else wide


HELD = 17
COPIED = 11


def start_all(copies):
    for copy in copies:
        copy.start()


def first_kernel(queue_ref, embed_hbm, pos_hbm, piece_ref, keep_ref, send_ref, embed_ref, pos_ref, sems):
    frames, _, tokens = queue_ref.shape
    shard, section = lax.axis_index("space"), lax.axis_index("tm")
    first = pl.multiple_of(shard * tokens, 8)
    copies = [
        pltpu.make_async_copy(embed_hbm, embed_ref, sems.at[0]),
        pltpu.make_async_copy(pos_hbm.at[pl.ds(first, tokens)], pos_ref, sems.at[1]),
    ]
    start_all(copies)
    own = tokens // 2
    lat = jnp.zeros((CH, LANES), f32)
    halves = [jnp.zeros((CH, LANES), f32) for _ in range(2)]
    for g in range(frames):
        block = queue_ref[g]
        lat = lat + placed(block, g * tokens)
        for half in range(2):
            halves[half] = halves[half] + placed(block[:, half * own : (half + 1) * own], g * own)
    low = section == 0
    keep_ref[...] = jnp.where(low, halves[0], pltpu.roll(halves[1], frames * own, 1))
    send_ref[...] = jnp.where(low, halves[1], pltpu.roll(halves[0], frames * own, 1))
    for copy in copies:
        copy.wait()
    piece = make_piece(lat, embed_ref[...], pos_ref[...])
    for peer in range(piece_ref.shape[0]):
        piece_ref[peer] = piece


def build_plans(mods_ref, pos_ref, embed_ref, weight_ref, left_ref, key_plan_ref, value_plan_ref):
    blocks, slots = key_plan_ref.shape[:2]
    tokens = LANES
    embed = embed_ref[...]
    embed = embed - jnp.mean(embed, axis=-1, keepdims=True)
    row = lax.broadcasted_iota(jnp.int32, (PIECE - CH, 1), 0)
    part = lax.broadcasted_iota(jnp.int32, (PIECE, 1), 0)
    lane = lax.broadcasted_iota(jnp.int32, (1, PIECE), 1)
    plan_row = lax.broadcasted_iota(jnp.int32, (PLAN, LANES), 0)
    deviation_columns = ((plan_row == tokens + CH + 1) | (plan_row == tokens + CH + 2)).astype(bf16)
    for b in range(blocks):
        pos = pos_ref[b * tokens : (b + 1) * tokens]
        pos = pos - jnp.mean(pos, axis=-1, keepdims=True)
        for q in range(slots):
            scale = 1.0 + mods_ref[q, 1:2]
            shift_rows = jnp.where(row < 3, mods_ref[q, 0:1], 0.0)
            left_ref[q * PLAN : (q + 1) * PLAN] = jnp.concatenate(
                [pos * scale, embed * scale, shift_rows], axis=0
            ).astype(bf16)
        product = dot_nt(left_ref[...], weight_ref[:INNER])
        for q in range(slots):
            rows = product[q * PLAN : (q + 1) * PLAN]
            group = rows[tokens:]
            group = jnp.where(part == CH + 1, group - group.astype(bf16).astype(f32), group)
            key_plan_ref[b, q] = jnp.concatenate(
                [
                    jnp.concatenate([rows[:tokens].astype(bf16), group.astype(bf16)], axis=0),
                    jnp.zeros((PLAN, WIDE - INNER), bf16),
                    deviation_columns,
                ],
                axis=1,
            )
        for q in range(slots):
            product = dot_nt(weight_ref[INNER:], left_ref[q * PLAN : (q + 1) * PLAN])
            group = product[:, tokens:]
            group = jnp.where(lane == CH + 1, group - group.astype(bf16).astype(f32), group)
            value_plan_ref[b, q] = jnp.concatenate(
                [product[:, :tokens].astype(bf16), group.astype(bf16)], axis=1
            )


def gain_products(gains):
    products = jnp.concatenate(
        [gains[0:1] * gains[1:2], gains[2:3] * gains[3:4], jnp.zeros((6, HD), f32)], axis=0
    ) / math.sqrt(HD)
    place = lax.broadcasted_iota(jnp.int32, (HD, WIDE), 1)
    feature = lax.broadcasted_iota(jnp.int32, (HD, WIDE), 0)
    spread = ((place < INNER) & (lax.rem(place, HD) == feature)).astype(f32)
    return lax.dot_general(
        products, spread, (((1,), (0,)), ((), ())), preferred_element_type=f32, precision=lax.Precision.HIGHEST
    )


def step_kernel(levels_ref, pieces_ref, lat_ref, *refs, step):
    first, last = step == 0, step == STEPS - 1
    if first:
        more_ref, pos_hbm, table_hbm, gains_hbm, wsi_hbm = refs[:5]
        sources = refs[5 : 5 + COPIED]
        outs = refs[5 + COPIED : 7 + COPIED]
        held = refs[7 + COPIED : 7 + COPIED + HELD]
        cross_ref, mixed_ref, pos_ref, gains_ref, weight_ref, left_ref, sems = refs[7 + COPIED + HELD :]
    else:
        held, outs, (cross_ref, mixed_ref) = refs[:HELD], refs[HELD : HELD + 2], refs[HELD + 2 :]
    (
        key_plan_ref,
        value_plan_ref,
        mods_ref,
        gain_rows_ref,
        pos_own_ref,
        wsi_ref,
        same_head_ref,
        embed_ref,
        head_sum_ref,
        own_head_ref,
        gather_ref,
        pos_frame_ref,
        noise_ref,
        final_ref,
        wso_ref,
        wti_ref,
        wto_ref,
    ) = held
    lanes = lat_ref.shape[1]
    blocks, slots = key_plan_ref.shape[:2]
    frames = slots * FRAMES
    own = lanes // frames
    devices = pieces_ref.shape[0]
    tokens = LANES
    per_block = devices // blocks
    section, sections = lax.axis_index("tm"), lax.axis_size("tm")

    if first:
        first_token = pl.multiple_of((lax.axis_index("space") * sections + section) * own, 8)
        early = [(table_hbm.at[levels_ref[q]], mods_ref.at[q]) for q in range(slots)]
        early += [(pos_hbm, pos_ref), (sources[1], embed_ref), (wsi_hbm.at[INNER:], weight_ref)]
        late = [
            (gains_hbm, gains_ref),
            (pos_hbm.at[pl.ds(first_token, own)], pos_own_ref),
            (wsi_hbm.at[:WIDE], wsi_ref),
        ]
        late += [pair for pair in zip(sources, held[6:]) if pair[1] is not embed_ref]
        copies = [pltpu.make_async_copy(*pair, sems.at[i]) for i, pair in enumerate(early + late)]
        early, late = copies[: len(early)], copies[len(early) :]
        start_all(early)
        for copy in early:
            copy.wait()
        start_all(late)
        build_plans(mods_ref, pos_ref, embed_ref, weight_ref, left_ref, key_plan_ref, value_plan_ref)
        for copy in late:
            copy.wait()
        gain_rows_ref[...] = gain_products(gains_ref[...])

    lat = lat_ref[...] + more_ref[...] if first else lat_ref[...]
    embed = embed_ref[...]
    pos_own = pos_own_ref[...]
    mods = [mods_ref[:, row] for row in range(8)]
    hidden = own_hidden(lat, embed, pos_own)
    normed = modulated(normalized(hidden), mods[0], mods[1]).astype(bf16)
    same_head = same_head_ref[...]

    def head_normed(values, gain):
        values = values.astype(bf16).astype(f32)
        total = dot((values * values).astype(bf16), same_head)
        return values * lax.rsqrt(total * (1.0 / HD) + epsilon) * gain

    queries = head_normed(dot_nt(normed, wsi_ref[...]), gain_rows_ref[0:1])

    for group in range(devices // PACK):
        stacked = pieces_ref[group * PACK : (group + 1) * PACK].astype(f32).reshape(LANES, lanes).T
        for part in range(PACK):
            cross_ref[group * PACK + part] = pltpu.roll(stacked, LANES - part * PIECE, 1) if part else stacked

    def turned(b, g):
        if first:
            held, rows = frames // sections, own * sections
            peers = range(b * per_block + g // held, (b + 1) * per_block, sections)
            at = g % held * rows
        else:
            rows, peers, at = own, range(b * per_block, (b + 1) * per_block), g * own
        return [cross_ref[peer, at : at + rows] for peer in peers]

    row = lax.broadcasted_iota(jnp.int32, (FRAMES * tokens, tokens), 0)
    column = lax.broadcasted_iota(jnp.int32, (FRAMES * tokens, tokens), 1)
    identity = (lax.rem(row, tokens) == column).astype(bf16)
    same_frame = (row // tokens == column // (HEADS * own)).astype(f32)
    masks = head_masks()
    head_sum = head_sum_ref[...]
    own_head = own_head_ref[...]

    for q in range(slots):
        spread = jnp.concatenate(
            [
                (queries[g * own : (g + 1) * own][None] * masks).reshape(HEADS * own, WIDE)
                for g in range(q * FRAMES, (q + 1) * FRAMES)
            ],
            axis=0,
        ).astype(bf16)
        total, mixed = 0.0, 0.0
        for b in range(blocks):
            tiles = [tile for f in range(FRAMES) for tile in turned(b, q * FRAMES + f)]
            left = jnp.concatenate([identity, jnp.concatenate(tiles, axis=0).astype(bf16)[:, :PIECE]], axis=1)
            product = dot(left, key_plan_ref[b, q])
            values = dot_nt(value_plan_ref[b, q], left).astype(bf16)
            deviation = product[:, WIDE:]
            keys = product[:, :WIDE]
            key_scale = lax.rsqrt(
                dot((keys * keys).astype(bf16), head_sum) * (1.0 / HD) + epsilon * deviation * deviation
            )
            scores = dot_nt(keys.astype(bf16), spread)
            weights = jnp.exp(scores * key_scale) * same_frame
            total = total + jnp.sum(weights, axis=0, keepdims=True)
            mixed = mixed + dot(values, (weights / deviation).astype(bf16))
        mixed_ref[:, q * LANES : (q + 1) * LANES] = (mixed * (1.0 / total) * own_head).astype(bf16)
    mixed = dot(mixed_ref[...], gather_ref[...]).T.astype(bf16)

    branch = dot(mixed, wso_ref[...])
    hidden = (
        hidden.reshape(slots, FRAMES, own, D)
        + mods[2][:, None, None, :] * branch.reshape(slots, FRAMES, own, D)
        + pos_frame_ref[...].reshape(slots, FRAMES, 1, D)
    ).reshape(lanes, D)
    normed = modulated(normalized(hidden), mods[3], mods[4]).astype(bf16)
    queries = head_normed(dot_nt(normed, wti_ref[:WIDE]), gain_rows_ref[1:2])
    keys = head_normed(dot_nt(normed, wti_ref[INNER : INNER + WIDE]), 1.0).astype(bf16)
    values = dot_nt(normed, wti_ref[2 * INNER :]).astype(bf16)
    row = lax.broadcasted_iota(jnp.int32, (lanes, lanes), 0)
    column = lax.broadcasted_iota(jnp.int32, (lanes, lanes), 1)
    same_token = (lax.rem(row, own) == lax.rem(column, own)).astype(f32)
    parts = [None] * (WIDE // LANES)
    for h in range(HEADS):
        start, stop = h * HD // LANES * LANES, -(-(h + 1) * HD // LANES) * LANES
        spread = (queries[:, start:stop] * masks[h, :, start:stop]).astype(bf16)
        weights = jnp.exp(dot_nt(spread, keys[:, start:stop])) * same_token
        total = jnp.sum(weights, axis=-1, keepdims=True)
        stop = min(stop, INNER)
        result = dot(weights.astype(bf16), values[:, start:stop]) * (1.0 / total) * masks[h, :, start:stop]
        for tile in range(start // LANES, -(-stop // LANES)):
            piece = result[:, tile * LANES - start : min((tile + 1) * LANES, stop) - start]
            parts[tile] = piece if parts[tile] is None else parts[tile] + piece
    mixed = jnp.concatenate([p.astype(bf16) for p in parts], axis=1)
    branch = dot(mixed, wto_ref[...])
    hidden = hidden + (mods[5][:, None, :] * branch.reshape(slots, FRAMES * own, D)).reshape(lanes, D)
    final = modulated(normalized(hidden), mods[6], mods[7])
    final_high, final_low = split(final)
    weight_high, weight_low = split(final_ref[...])
    velocity = dot_nt(weight_high, final_high) + dot_nt(weight_low, final_high) + dot_nt(weight_high, final_low)

    slot = lax.broadcasted_iota(jnp.int32, (1, lanes), 1) // (FRAMES * own)
    times = jnp.zeros((1, lanes), f32)
    stride = jnp.zeros((1, lanes), f32)
    before = 0.0
    for q in range(slots):
        time = (levels_ref[q].astype(f32) + 1.0) / LEVELS
        times = jnp.where(slot == q, time, times)
        stride = jnp.where(slot == q, time - before, stride)
        before = time
    low = section == 0
    noise = 0.0
    for f in range(FRAMES):
        block = noise_ref[step, f]
        block = jnp.where(low, block[:, :own], block[:, own:])
        noise = noise + placed(block, (frames - FRAMES + f) * own)
    moved = pltpu.roll(lat - stride * velocity, lanes - FRAMES * own, 1)
    moved = jnp.where(slot == slots - 1, noise, moved)
    if not last:
        lat_out, piece_out = outs
        lat_out[...] = moved
        piece = make_piece(moved, embed, pos_own)
        for peer in range(devices):
            piece_out[peer] = piece
    else:
        keep_out, send_out = outs
        held = frames // sections
        for i, result in enumerate((moved, lat - times * velocity)):
            for g in range(held):
                here = [
                    pltpu.roll(result, (lanes - (half * held + g) * own) % lanes, 1)[:, :own] for half in range(2)
                ]
                for out, block in (
                    (keep_out, jnp.where(low, here[0], here[1])),
                    (send_out, jnp.where(low, here[1], here[0])),
                ):
                    zeros = jnp.zeros_like(block)
                    out[i, g] = jnp.concatenate(
                        [jnp.where(low, block, zeros), jnp.where(low, zeros, block)], axis=1
                    )


def per_device(
    queue_latents,
    fresh_noise,
    slot_levels,
    level_table,
    embed_weight,
    spatial_in,
    spatial_out,
    temporal_in,
    temporal_out,
    norm_gains,
    final_weight,
):
    blocks, _, _, tokens = queue_latents.shape
    sections = lax.axis_size("tm")
    shards = lax.axis_size("space")
    axes = ("space", "tm")
    devices = sections * shards
    own = tokens // sections
    slots = blocks * sections
    frames = slots * FRAMES
    lanes = frames * own
    space_tokens = tokens * shards
    token_blocks = space_tokens // LANES
    partner = [(i, sections - 1 - i) for i in range(sections)]

    pos = jnp.asarray(sincos(space_tokens, D).astype(np.float32))
    pos_frame = jnp.asarray(sincos(frames, D).astype(np.float32))
    head = np.where(np.arange(WIDE) < INNER, np.arange(WIDE) // HD, -1)
    same_head = jnp.asarray(((head[:, None] == head[None, :]) & (head >= 0)[None, :]).astype(np.float32), bf16)
    lane = np.arange(LANES)
    lane_head = lane // own % HEADS
    head_sum = jnp.asarray((head[:, None] == lane_head[None, :]).astype(np.float32), bf16)
    own_head = jnp.asarray((head[:INNER, None] == lane_head[None, :]).astype(np.float32))
    packed = np.arange(slots * LANES)
    packed_lane = packed // (HEADS * own) * own + packed % own
    gather = jnp.asarray((packed_lane[:, None] == lane[None, :]).astype(np.float32), bf16)

    final_turned = jnp.transpose(final_weight)
    spatial_turned = jnp.transpose(spatial_in)
    temporal_turned = jnp.transpose(temporal_in)

    vmem = pl.BlockSpec(memory_space=pltpu.VMEM)
    smem = pl.BlockSpec(memory_space=pltpu.SMEM)
    hbm = pl.BlockSpec(memory_space=pltpu.HBM)
    dma = pltpu.SemaphoreType.DMA

    def call(kernel, out_shape, arguments, scratch, name):
        spaces = {id(vmem): pltpu.VMEM, id(hbm): pltpu.HBM}
        values = [
            pltpu.with_memory_space_constraint(value, spaces[id(spec)]) if id(spec) in spaces else value
            for value, spec in arguments
        ]
        return pl.pallas_call(
            kernel,
            out_shape=out_shape,
            in_specs=[spec for _, spec in arguments],
            out_specs=[vmem] * len(out_shape),
            scratch_shapes=scratch,
            compiler_params=pltpu.CompilerParams(vmem_limit_bytes=GRANT),
            name=name,
        )(*values)

    flat = pltpu.VMEM((CH, lanes), f32)
    piece_shape = pltpu.VMEM((devices, PIECE, lanes), bf16)
    pieces, lat, send = call(
        first_kernel,
        [piece_shape, flat, flat],
        [(queue_latents.reshape(blocks * FRAMES, CH, tokens), vmem), (embed_weight, hbm), (pos, hbm)],
        [pltpu.VMEM((CH, D), f32), pltpu.VMEM((tokens, D), f32), dma((2,))],
        "first_piece",
    )
    more = lax.ppermute(send, "tm", partner)

    copied = [
        same_head,
        embed_weight,
        head_sum,
        own_head,
        gather,
        pos_frame,
        fresh_noise,
        final_turned,
        spatial_out,
        temporal_turned,
        temporal_out,
    ]
    held = [
        pltpu.VMEM((token_blocks, slots, PLAN, WIDE + LANES), bf16),
        pltpu.VMEM((token_blocks, slots, INNER, PLAN), bf16),
        pltpu.VMEM((slots, 8, D), f32),
        pltpu.VMEM((8, WIDE), f32),
        pltpu.VMEM((own, D), f32),
        pltpu.VMEM((WIDE, D), bf16),
        *(pltpu.VMEM(x.shape, x.dtype) for x in copied),
    ]
    result_shape = pltpu.VMEM((2, blocks * FRAMES, CH, tokens), f32)
    for step in range(STEPS):
        first, last = step == 0, step == STEPS - 1
        gathered = lax.all_to_all(pieces, axes, split_axis=0, concat_axis=0, tiled=True)
        out_shape = [result_shape] * 2 if last else [flat, piece_shape]
        arguments = [(slot_levels, smem), (gathered, vmem), (lat, vmem)]
        scratch = [pltpu.VMEM((devices, lanes, LANES), f32), pltpu.VMEM((INNER, slots * LANES), bf16)]
        if first:
            arguments += [(more, vmem)]
            arguments += [(x, hbm) for x in (pos, level_table, norm_gains, spatial_turned, *copied)]
            out_shape = out_shape + held
            scratch += [
                pltpu.VMEM((space_tokens, D), f32),
                pltpu.VMEM((4, HD), f32),
                pltpu.VMEM((2 * INNER, D), bf16),
                pltpu.VMEM((slots * PLAN, D), bf16),
                dma((slots + 3 + 3 + COPIED,)),
            ]
        else:
            arguments += [(x, vmem) for x in held]
        lat, pieces, *made = call(
            functools.partial(step_kernel, step=step), out_shape, arguments, scratch, "denoise_step"
        )
        held = made if first else held

    received = lax.ppermute(pieces, "tm", partner)
    return tuple((lat[i] + received[i]).reshape(queue_latents.shape) for i in range(2))


def solution(mesh):
    return jax.shard_map(
        per_device,
        mesh=mesh,
        in_specs=(
            P(("clip", "tm"), None, None, "space"),
            P("clip", None, None, "space"),
            P("clip"),
            P(),
            P(),
            P(),
            P(),
            P(),
            P(),
            P(),
            P(),
        ),
        out_specs=(P(("clip", "tm"), None, None, "space"), P(("clip", "tm"), None, None, "space")),
        check_vma=False,
    )
```

profile of v0, /device:TPU:0, one launch (start us, length us, event | category | flops | bytes accessed | tf_op | source)
XLA Modules:
  0.0 87.5 jit_solution(4835934408497439864)
XLA Ops:
  0.6 0.0 copy-start
  0.6 0.8 copy-done
  1.5 2.2 %first_piece.1 = (bf16[16,32,128]{2,1,0:T(8,128)(2,1)}, f32[16,128]{1,0:T(8,128)S(1)}, f32[16,128]{1,0:T(8,128)S(1)}) custom-call(f32[8,16,16]{2,1,0:T(8,128)S(1)} %bitcast.6, f32[16,1152]{1,0:T(8,128)} %refs_6_.1, f32[128,1152]{1,0:T(8,128)} %constant.12.clone.pos_hbm.refs_1_), custom_call_target="tpu_custom_call" | custom-call | tf_op jit(solution)/shard_map/first_piece/pallas_call | solution.py:441
  3.7 7.4 %all-to-all-start = ((bf16[16,32,128]{2,1,0:T(8,128)(2,1)}), bf16[16,32,128]{2,1,0:T(8,128)(2,1)S(1)}, u32[]{:S(2)}, u32[]{:S(2)}) async-start(bf16[16,32,128]{2,1,0:T(8,128)(2,1)} %get-tuple-element.28), calls=%async_computation | async-start | bytes 262144 | tf_op jit(solution)/shard_map/all_to_all | solution.py:487
  11.1 0.4 collective-permute-start
  11.5 0.8 collective-permute-done.refs_0_
  12.3 6.7 %all-to-all-done.pieces_ref = bf16[16,32,128]{2,1,0:T(8,128)(2,1)S(1)} async-done(((bf16[16,32,128]{2,1,0:T(8,128)(2,1)}), bf16[16,32,128]{2,1,0:T(8,128)(2,1)S(1)}, u32[]{:S(2)}, u32[]{:S(2)}) %all-to-all-start) | async-done | bytes 131104 | tf_op jit(solution)/shard_map/all_to_all | solution.py:487
  19.0 0.0 copy-start.1
  19.0 0.7 copy-done.1
  19.7 20.9 %denoise_step.3 = (f32[16,128]{1,0:T(8,128)S(1)}, bf16[16,32,128]{2,1,0:T(8,128)(2,1)S(1)}, bf16[1,8,160,768]{3,2,1,0:T(8,128)(2,1)S(1)}, bf16[1,8,576,160]{3,2,...) custom-call(s32[8]{0:T(128)S(1)} %copy-done.1, ...), custom_call_target="tpu_custom_call" | custom-call | tf_op jit(solution)/shard_map/denoise_step/pallas_call | solution.py:441
  40.6 10.5 %all_to_all.15.pieces_ref = bf16[16,32,128]{2,1,0:T(8,128)(2,1)S(1)} all-to-all(bf16[16,32,128]{2,1,0:T(8,128)(2,1)S(1)} %get-tuple-element.31), channel_id=1, replica_groups=mesh['clip'=2,'tm'=2,'space'=8] {'space','tm'}, dimensions={0} | all-to-all | bytes 262144 | tf_op jit(solution)/shard_map/all_to_all | solution.py:487
  51.1 12.1 %denoise_step.4 = (f32[16,128]{1,0:T(8,128)S(1)}, bf16[16,32,128]{2,1,0:T(8,128)(2,1)S(1)}) custom-call(s32[8]{0:T(128)S(1)} %copy-done.1, bf16[16,32,128]{2,1,0:T(8,128)(2,1)S(1)} %all_to_all.15.pieces_ref, f32[16,128]{1,0:T(8,128)S(1)} %get-tuple-element.32.lat_ref, bf16[1,8,160,768]{3,2,1,0:T(8,128)(2,1)S(1)} %get-tuple-element.33.refs_0_, ...), custom_call_target="tpu_custom_call" | custom-call | tf_op jit(solution)/shard_map/denoise_step/pallas_call | solution.py:441
  63.3 10.5 %all_to_all.16.pieces_ref = bf16[16,32,128]{2,1,0:T(8,128)(2,1)S(1)} all-to-all(bf16[16,32,128]{2,1,0:T(8,128)(2,1)S(1)} %get-tuple-element.50), channel_id=1, replica_groups=mesh['clip'=2,'tm'=2,'space'=8] {'space','tm'}, dimensions={0} | all-to-all | bytes 262144 | tf_op jit(solution)/shard_map/all_to_all | solution.py:487
  73.8 11.7 %denoise_step.5 = (f32[2,8,16,16]{3,2,1,0:T(8,128)S(1)}, f32[2,8,16,16]{3,2,1,0:T(8,128)S(1)}) custom-call(s32[8]{0:T(128)S(1)} %copy-done.1, bf16[16,32,128]{2,1,0:T(8,128)(2,1)S(1)} %all_to_all.16.pieces_ref, f32[16,128]{1,0:T(8,128)S(1)} %get-tuple-element.51.lat_ref, bf16[1,8,160,768]{3,2,1,0:T(8,128)(2,1)S(1)} %get-tuple-element.33.refs_0_, ...), custom_call_target="tpu_custom_call" | custom-call | tf_op jit(solution)/shard_map/denoise_step/pallas_call | solution.py:441
  85.4 0.1 collective-permute-start.1
  85.5 1.3 %collective-permute-done.1 = f32[2,8,16,16]{3,2,1,0:T(8,128)S(1)} collective-permute-done((f32[2,8,16,16]{3,2,1,0:T(8,128)S(1)}, f32[2,8,16,16]{3,2,1,0:T(8,128)S(1)}, u32[]{:S(2)}, u32[]{:S(2)}) %collective-permute-start.1) | collective-permute-done | bytes 16416 | tf_op jit(solution)/shard_map/ppermute | solution.py:509
  86.9 0.7 slice_add_fusion
Async XLA Ops:
  0.6 0.8 copy-start
  3.7 15.3 %all-to-all-start = ((bf16[16,32,128]{2,1,0:T(8,128)(2,1)}), bf16[16,32,128]{2,1,0:T(8,128)(2,1)S(1)}, u32[]{:S(2)}, u32[]{:S(2)}) async-start(bf16[16,32,128]{2,1,0:T(8,128)(2,1)} %get-tuple-element.28), calls=%async_computation | async-start | bytes 262144 | tf_op jit(solution)/shard_map/all_to_all | solution.py:487
  11.1 1.2 %collective-permute-start = (f32[16,128]{1,0:T(8,128)S(1)}, f32[16,128]{1,0:T(8,128)S(1)}, u32[]{:S(2)}, u32[]{:S(2)}) collective-permute-start(f32[16,128]{1,0:T(8,128)S(1)} %get-tuple-element.30), channel_id=1, source_target_pairs={{0,8},{8,0},{1,9},{9,1},{2,10},{10,2},{3,11},{11,3},{4,12},{12,4},... | collective-permute-start | bytes 24584 | tf_op jit(solution)/shard_map/ppermute | solution.py:460
  19.0 0.7 copy-start.1
  85.4 1.4 %collective-permute-start.1 = (f32[2,8,16,16]{3,2,1,0:T(8,128)S(1)}, f32[2,8,16,16]{3,2,1,0:T(8,128)S(1)}, u32[]{:S(2)}, u32[]{:S(2)}) collective-permute-start(f32[2,8,16,16]{3,2,1,0:T(8,128)S(1)} %get-tuple-element.53), channel_id=1, source_target_pairs={{0,8},{8,0},{1,9},{9,1},{2,10},{10,2},{3,11},{11,3},{4,12},{12,4},... | collective-permute-start | bytes 49160 | tf_op jit(solution)/shard_map/ppermute | solution.py:509
where the time goes:
time: 87.9 us; the launch traced here: 87.5 us
  Pallas kernels  46.9 us (53%)
  blocking collectives  21 us (24%)
  waiting for transfers between devices  8.86 us (10%)
  starting transfers between devices  7.88 us (9%)
  local copies, waits for them, and re-layouts  1.49 us (2%)
    pallas_call x4, Pallas kernels, call(): pl.pallas_call(kernel, out_shape=out_shape, in_specs=[spec for _, spec in...  46.9 us
    all_to_all x2, blocking collectives, per_device(): lax.all_to_all(pieces, axes, split_axis=0, concat_axis=0, tiled=True)  21 us
    all_to_all x1, starting transfers between devices, per_device(): lax.all_to_all(pieces, axes, split_axis=0, concat_axis=0, tiled=True)  7.4 us
    all_to_all x1, waiting for transfers between devices, per_device(): lax.all_to_all(pieces, axes, split_axis=0, concat_axis=0, tiled=True)  6.7 us
  transfers between devices with their start and end apart: 3, of which 3 were waited for; matrix products, arithmetic and copies ran while one was open for 0% of the time, Pallas kernels for 0%

commit v1 on v0

--- a/solution.py
+++ b/solution.py
@@ -83,16 +83,16 @@
     return (dot(rows, weights).reshape(lanes // own, own, D) + pos_own[None]).reshape(lanes, D)
 
 
-def make_piece(lat, embed, pos_own):
+def make_piece(lat, hidden, rest=None):
     lanes = lat.shape[1]
-    hidden = own_hidden(lat, embed, pos_own)
     centered = hidden - jnp.mean(hidden, axis=-1, keepdims=True)
     deviation = jnp.sqrt(jnp.mean(centered * centered, axis=-1, keepdims=True) + epsilon)
     row = jnp.broadcast_to(deviation, (lanes, LANES)).T[:1]
     high, low = split(row)
     high = high.astype(f32)
-    zeros = jnp.zeros((PIECE - CH - 3, lanes), f32)
-    return jnp.concatenate([lat, high, high, low.astype(f32), zeros], axis=0).astype(bf16)
+    rest = jnp.zeros((CH // 2, lanes), f32) if rest is None else rest
+    zeros = jnp.zeros((PIECE - CH - 3 - CH // 2, lanes), f32)
+    return jnp.concatenate([lat, high, high, low.astype(f32), zeros, rest], axis=0).astype(bf16)
 
 
 def placed(block, start):
@@ -108,33 +108,6 @@
 def start_all(copies):
     for copy in copies:
         copy.start()
-
-
-def first_kernel(queue_ref, embed_hbm, pos_hbm, piece_ref, keep_ref, send_ref, embed_ref, pos_ref, sems):
-    frames, _, tokens = queue_ref.shape
-    shard, section = lax.axis_index("space"), lax.axis_index("tm")
-    first = pl.multiple_of(shard * tokens, 8)
-    copies = [
-        pltpu.make_async_copy(embed_hbm, embed_ref, sems.at[0]),
-        pltpu.make_async_copy(pos_hbm.at[pl.ds(first, tokens)], pos_ref, sems.at[1]),
-    ]
-    start_all(copies)
-    own = tokens // 2
-    lat = jnp.zeros((CH, LANES), f32)
-    halves = [jnp.zeros((CH, LANES), f32) for _ in range(2)]
-    for g in range(frames):
-        block = queue_ref[g]
-        lat = lat + placed(block, g * tokens)
-        for half in range(2):
-            halves[half] = halves[half] + placed(block[:, half * own : (half + 1) * own], g * own)
-    low = section == 0
-    keep_ref[...] = jnp.where(low, halves[0], pltpu.roll(halves[1], frames * own, 1))
-    send_ref[...] = jnp.where(low, halves[1], pltpu.roll(halves[0], frames * own, 1))
-    for copy in copies:
-        copy.wait()
-    piece = make_piece(lat, embed_ref[...], pos_ref[...])
-    for peer in range(piece_ref.shape[0]):
-        piece_ref[peer] = piece
 
 
 def build_plans(mods_ref, pos_ref, embed_ref, weight_ref, left_ref, key_plan_ref, value_plan_ref):
@@ -190,16 +163,84 @@
     )
 
 
+def head_normed(values, same_head, gain):
+    values = values.astype(bf16).astype(f32)
+    total = dot((values * values).astype(bf16), same_head)
+    return values * lax.rsqrt(total * (1.0 / HD) + epsilon) * gain
+
+
+def low_rows(lat):
+    low = split(lat)[1].astype(f32)
+    half = lat.shape[0] // 2
+    return low[:half] + pltpu.roll(low[half:], LANES // 2, 1)
+
+
+def partner_latents(piece, held, tokens, low):
+    own = tokens // 2
+    lane = lax.broadcasted_iota(jnp.int32, (1, LANES), 1)
+    left = lane < LANES // 2
+    high = jnp.where(low, piece[:CH], pltpu.roll(piece[:CH], LANES - own, 1))
+    rest = piece[PIECE - CH // 2 :]
+    out = jnp.where(left, jnp.concatenate([rest, pltpu.roll(rest, LANES // 2, 1)], axis=0), 0.0)
+    for g in range(held):
+        moved = pltpu.roll(high, LANES - g * own, 1) if g else high
+        out = out + jnp.where(lane // own == g, moved, 0.0)
+    return jnp.where(low, pltpu.roll(out, LANES // 2, 1), out)
+
+
+def prepare_kernel(levels_ref, queue_hbm, pos_hbm, table_hbm, gains_hbm, wsi_hbm, *refs):
+    sources, held = refs[:COPIED], refs[COPIED : COPIED + HELD]
+    piece_ref, lat_ref, queue_ref, pos_ref, pos_shard_ref, gains_ref, weight_ref, left_ref, sems = refs[COPIED + HELD :]
+    key_plan_ref, value_plan_ref, mods_ref, gain_rows_ref, pos_own_ref, wsi_ref, same_head_ref, embed_ref = held[:8]
+    slots = mods_ref.shape[0]
+    frames, _, tokens = queue_ref.shape
+    own = pos_own_ref.shape[0]
+    section, sections = lax.axis_index("tm"), lax.axis_size("tm")
+    shard_token = pl.multiple_of(lax.axis_index("space") * tokens, 8)
+    own_token = pl.multiple_of(shard_token + section * own, 8)
+    stages = [
+        [(queue_hbm, queue_ref), (sources[1], embed_ref), (pos_hbm.at[pl.ds(shard_token, tokens)], pos_shard_ref)],
+        [(table_hbm.at[levels_ref[q]], mods_ref.at[q]) for q in range(slots)]
+        + [(pos_hbm, pos_ref), (wsi_hbm.at[INNER:], weight_ref)],
+        [
+            (gains_hbm, gains_ref),
+            (pos_hbm.at[pl.ds(own_token, own)], pos_own_ref),
+            (wsi_hbm.at[:WIDE], wsi_ref),
+        ]
+        + [pair for pair in zip(sources, held[6:]) if pair[1] is not embed_ref],
+    ]
+    count = 0
+    for i, stage in enumerate(stages):
+        stages[i] = [pltpu.make_async_copy(*pair, sems.at[count + j]) for j, pair in enumerate(stage)]
+        count += len(stage)
+    start_all(stages[0] + stages[1])
+    for copy in stages[0]:
+        copy.wait()
+    lat = jnp.zeros((CH, LANES), f32)
+    halves = [jnp.zeros((CH, LANES), f32) for _ in range(2)]
+    for g in range(frames):
+        block = queue_ref[g]
+        lat = lat + placed(block, g * tokens)
+        for half in range(2):
+            halves[half] = halves[half] + placed(block[:, half * own : (half + 1) * own], g * own)
+    low = section == 0
+    lat_ref[...] = jnp.where(low, halves[0], pltpu.roll(halves[1], LANES // 2, 1))
+    rest = low_rows(jnp.where(low, halves[1], halves[0]))
+    piece = make_piece(lat, own_hidden(lat, embed_ref[...], pos_shard_ref[...]), rest)
+    for peer in range(piece_ref.shape[0]):
+        piece_ref[peer] = piece
+    for copy in stages[1]:
+        copy.wait()
+    start_all(stages[2])
+    build_plans(mods_ref, pos_ref, embed_ref, weight_ref, left_ref, key_plan_ref, value_plan_ref)
+    for copy in stages[2]:
+        copy.wait()
+    gain_rows_ref[...] = gain_products(gains_ref[...])
+
+
 def step_kernel(levels_ref, pieces_ref, lat_ref, *refs, step):
     first, last = step == 0, step == STEPS - 1
-    if first:
-        more_ref, pos_hbm, table_hbm, gains_hbm, wsi_hbm = refs[:5]
-        sources = refs[5 : 5 + COPIED]
-        outs = refs[5 + COPIED : 7 + COPIED]
-        held = refs[7 + COPIED : 7 + COPIED + HELD]
-        cross_ref, mixed_ref, pos_ref, gains_ref, weight_ref, left_ref, sems = refs[7 + COPIED + HELD :]
-    else:
-        held, outs, (cross_ref, mixed_ref) = refs[:HELD], refs[HELD : HELD + 2], refs[HELD + 2 :]
+    outs, (cross_ref, mixed_ref) = refs[HELD:-2], refs[-2:]
     (
         key_plan_ref,
         value_plan_ref,
@@ -218,7 +259,7 @@
         wso_ref,
         wti_ref,
         wto_ref,
-    ) = held
+    ) = refs[:HELD]
     lanes = lat_ref.shape[1]
     blocks, slots = key_plan_ref.shape[:2]
     frames = slots * FRAMES
@@ -227,42 +268,17 @@
     tokens = LANES
     per_block = devices // blocks
     section, sections = lax.axis_index("tm"), lax.axis_size("tm")
-
+    low = section == 0
+    mods = [mods_ref[:, row] for row in range(8)]
+    same_head = same_head_ref[...]
+
+    lat = lat_ref[...]
     if first:
-        first_token = pl.multiple_of((lax.axis_index("space") * sections + section) * own, 8)
-        early = [(table_hbm.at[levels_ref[q]], mods_ref.at[q]) for q in range(slots)]
-        early += [(pos_hbm, pos_ref), (sources[1], embed_ref), (wsi_hbm.at[INNER:], weight_ref)]
-        late = [
-            (gains_hbm, gains_ref),
-            (pos_hbm.at[pl.ds(first_token, own)], pos_own_ref),
-            (wsi_hbm.at[:WIDE], wsi_ref),
-        ]
-        late += [pair for pair in zip(sources, held[6:]) if pair[1] is not embed_ref]
-        copies = [pltpu.make_async_copy(*pair, sems.at[i]) for i, pair in enumerate(early + late)]
-        early, late = copies[: len(early)], copies[len(early) :]
-        start_all(early)
-        for copy in early:
-            copy.wait()
-        start_all(late)
-        build_plans(mods_ref, pos_ref, embed_ref, weight_ref, left_ref, key_plan_ref, value_plan_ref)
-        for copy in late:
-            copy.wait()
-        gain_rows_ref[...] = gain_products(gains_ref[...])
-
-    lat = lat_ref[...] + more_ref[...] if first else lat_ref[...]
-    embed = embed_ref[...]
-    pos_own = pos_own_ref[...]
-    mods = [mods_ref[:, row] for row in range(8)]
-    hidden = own_hidden(lat, embed, pos_own)
+        partner = lax.axis_index("space") * sections + (sections - 1 - section)
+        lat = lat + partner_latents(pieces_ref[partner].astype(f32), frames // sections, own * sections, low)
+    hidden = own_hidden(lat, embed_ref[...], pos_own_ref[...])
     normed = modulated(normalized(hidden), mods[0], mods[1]).astype(bf16)
-    same_head = same_head_ref[...]
-
-    def head_normed(values, gain):
-        values = values.astype(bf16).astype(f32)
-        total = dot((values * values).astype(bf16), same_head)
-        return values * lax.rsqrt(total * (1.0 / HD) + epsilon) * gain
-
-    queries = head_normed(dot_nt(normed, wsi_ref[...]), gain_rows_ref[0:1])
+    queries = head_normed(dot_nt(normed, wsi_ref[...]), same_head, gain_rows_ref[0:1])
 
     for group in range(devices // PACK):
         stacked = pieces_ref[group * PACK : (group + 1) * PACK].astype(f32).reshape(LANES, lanes).T
@@ -319,8 +335,8 @@
         + pos_frame_ref[...].reshape(slots, FRAMES, 1, D)
     ).reshape(lanes, D)
     normed = modulated(normalized(hidden), mods[3], mods[4]).astype(bf16)
-    queries = head_normed(dot_nt(normed, wti_ref[:WIDE]), gain_rows_ref[1:2])
-    keys = head_normed(dot_nt(normed, wti_ref[INNER : INNER + WIDE]), 1.0).astype(bf16)
+    queries = head_normed(dot_nt(normed, wti_ref[:WIDE]), same_head, gain_rows_ref[1:2])
+    keys = head_normed(dot_nt(normed, wti_ref[INNER : INNER + WIDE]), same_head, 1.0).astype(bf16)
     values = dot_nt(normed, wti_ref[2 * INNER :]).astype(bf16)
     row = lax.broadcasted_iota(jnp.int32, (lanes, lanes), 0)
     column = lax.broadcasted_iota(jnp.int32, (lanes, lanes), 1)
@@ -353,7 +369,6 @@
         times = jnp.where(slot == q, time, times)
         stride = jnp.where(slot == q, time - before, stride)
         before = time
-    low = section == 0
     noise = 0.0
     for f in range(FRAMES):
         block = noise_ref[step, f]
@@ -364,7 +379,7 @@
     if not last:
         lat_out, piece_out = outs
         lat_out[...] = moved
-        piece = make_piece(moved, embed, pos_own)
+        piece = make_piece(moved, own_hidden(moved, embed_ref[...], pos_own_ref[...]))
         for peer in range(devices):
             piece_out[peer] = piece
     else:
@@ -450,15 +465,7 @@
 
     flat = pltpu.VMEM((CH, lanes), f32)
     piece_shape = pltpu.VMEM((devices, PIECE, lanes), bf16)
-    pieces, lat, send = call(
-        first_kernel,
-        [piece_shape, flat, flat],
-        [(queue_latents.reshape(blocks * FRAMES, CH, tokens), vmem), (embed_weight, hbm), (pos, hbm)],
-        [pltpu.VMEM((CH, D), f32), pltpu.VMEM((tokens, D), f32), dma((2,))],
-        "first_piece",
-    )
-    more = lax.ppermute(send, "tm", partner)
-
+    queue = queue_latents.reshape(blocks * FRAMES, CH, tokens)
     copied = [
         same_head,
         embed_weight,
@@ -481,30 +488,33 @@
         pltpu.VMEM((WIDE, D), bf16),
         *(pltpu.VMEM(x.shape, x.dtype) for x in copied),
     ]
+    *held, pieces, lat = call(
+        prepare_kernel,
+        held + [piece_shape, flat],
+        [(slot_levels, smem)]
+        + [(x, hbm) for x in (queue, pos, level_table, norm_gains, spatial_turned, *copied)],
+        [
+            pltpu.VMEM(queue.shape, f32),
+            pltpu.VMEM((space_tokens, D), f32),
+            pltpu.VMEM((tokens, D), f32),
+            pltpu.VMEM((4, HD), f32),
+            pltpu.VMEM((2 * INNER, D), bf16),
+            pltpu.VMEM((slots * PLAN, D), bf16),
+            dma((3 + slots + 2 + 3 + COPIED,)),
+        ],
+        "slot_plan",
+    )
     result_shape = pltpu.VMEM((2, blocks * FRAMES, CH, tokens), f32)
     for step in range(STEPS):
-        first, last = step == 0, step == STEPS - 1
+        last = step == STEPS - 1
         gathered = lax.all_to_all(pieces, axes, split_axis=0, concat_axis=0, tiled=True)
-        out_shape = [result_shape] * 2 if last else [flat, piece_shape]
-        arguments = [(slot_levels, smem), (gathered, vmem), (lat, vmem)]
-        scratch = [pltpu.VMEM((devices, lanes, LANES), f32), pltpu.VMEM((INNER, slots * LANES), bf16)]
-        if first:
-            arguments += [(more, vmem)]
-            arguments += [(x, hbm) for x in (pos, level_table, norm_gains, spatial_turned, *copied)]
-            out_shape = out_shape + held
-            scratch += [
-                pltpu.VMEM((space_tokens, D), f32),
-                pltpu.VMEM((4, HD), f32),
-                pltpu.VMEM((2 * INNER, D), bf16),
-                pltpu.VMEM((slots * PLAN, D), bf16),
-                dma((slots + 3 + 3 + COPIED,)),
-            ]
-        else:
-            arguments += [(x, vmem) for x in held]
-        lat, pieces, *made = call(
-            functools.partial(step_kernel, step=step), out_shape, arguments, scratch, "denoise_step"
+        lat, pieces = call(
+            functools.partial(step_kernel, step=step),
+            [result_shape] * 2 if last else [flat, piece_shape],
+            [(slot_levels, smem)] + [(x, vmem) for x in (gathered, lat, *held)],
+            [pltpu.VMEM((devices, lanes, LANES), f32), pltpu.VMEM((INNER, slots * LANES), bf16)],
+            "denoise_step",
         )
-        held = made if first else held
 
     received = lax.ppermute(pieces, "tm", partner)
     return tuple((lat[i] + received[i]).reshape(queue_latents.shape) for i in range(2))

time: 87.9 us -> 86.5 us (0.984)
  blocking collectives: 21 us -> 36.2 us
  starting transfers between devices: 7.88 us -> 0.07 us
  waiting for transfers between devices: 8.86 us -> 1.33 us
    all_to_all x2 -> x3, blocking collectives: 21 us -> 36.2 us  [per_device(): lax.all_to_all(pieces, axes, split_axis=0, concat_axis=0, tiled=True)]
    all_to_all x1 -> x0, starting transfers between devices: 7.4 us -> none  [per_device(): lax.all_to_all(pieces, axes, split_axis=0, concat_axis=0, tiled=True)]
    all_to_all x1 -> x0, waiting for transfers between devices: 6.7 us -> none  [per_device(): lax.all_to_all(pieces, axes, split_axis=0, concat_axis=0, tiled=True)]
  transfers between devices with their start and end apart: 3 -> 1, of which waited for: 3 -> 1; matrix products, arithmetic and copies ran while one was open for 0% -> 0% of each run, Pallas kernels for 0% -> 0%
where the time goes in v1:
time: 86.5 us; the launch traced here: 86.3 us
  Pallas kernels  46.7 us (54%)
  blocking collectives  36.2 us (42%)
  waiting for transfers between devices  1.33 us (2%)
    pallas_call x4, Pallas kernels, call(): pl.pallas_call(kernel, out_shape=out_shape, in_specs=[spec for _, spec in...  46.7 us
    all_to_all x3, blocking collectives, per_device(): lax.all_to_all(pieces, axes, split_axis=0, concat_axis=0, tiled=True)  36.2 us
  transfers between devices with their start and end apart: 1, of which 1 were waited for; matrix products, arithmetic and copies ran while one was open for 0% of the time, Pallas kernels for 0%

profile of v1, /device:TPU:0, one launch (start us, length us, event | category | flops | bytes accessed | tf_op | source)
XLA Modules:
  0.0 86.3 jit_solution(10837172408412585281)
XLA Ops:
  0.6 0.0 copy-start
  0.6 0.6 copy-done
  1.3 10.6 %slot_plan.1 = (bf16[1,8,160,768]{3,2,1,0:T(8,128)(2,1)S(1)}, bf16[1,8,576,160]{3,2,1,0:T(8,128)(2,1)S(1)}, f32[8,8,1152]{2,1,0:T(8,128)S(1)}, f32[8,640]{1,0:T(...) custom-call(s32[8]{0:T(128)S(1)} %copy-done, ...), custom_call_target="tpu_custom_call" | custom-call | tf_op jit(solution)/shard_map/slot_plan/pallas_call | solution.py:456
  11.9 15.1 %all_to_all.15.pieces_ref = bf16[16,32,128]{2,1,0:T(8,128)(2,1)S(1)} all-to-all(bf16[16,32,128]{2,1,0:T(8,128)(2,1)S(1)} %get-tuple-element.27), channel_id=1, replica_groups=mesh['clip'=2,'tm'=2,'space'=8] {'space','tm'}, dimensions={0} | all-to-all | bytes 262144 | tf_op jit(solution)/shard_map/all_to_all | solution.py:510
  27.0 12.4 %denoise_step.3 = (f32[16,128]{1,0:T(8,128)S(1)}, bf16[16,32,128]{2,1,0:T(8,128)(2,1)S(1)}) custom-call(s32[8]{0:T(128)S(1)} %copy-done, bf16[16,32,128]{2,1,0:T(8,128)(2,1)S(1)} %all_to_all.15.pieces_ref, f32[16,128]{1,0:T(8,128)S(1)} %get-tuple-element.28.lat_ref, bf16[1,8,160,768]{3,2,1,0:T(8,128)(2,1)S(1)} %get-tuple-element.29.refs_0_, ...), custom_call_target="tpu_custom_call" | custom-call | tf_op jit(solution)/shard_map/denoise_step/pallas_call | solution.py:456
  39.4 10.5 %all_to_all.16.pieces_ref = bf16[16,32,128]{2,1,0:T(8,128)(2,1)S(1)} all-to-all(bf16[16,32,128]{2,1,0:T(8,128)(2,1)S(1)} %get-tuple-element.46), channel_id=1, replica_groups=mesh['clip'=2,'tm'=2,'space'=8] {'space','tm'}, dimensions={0} | all-to-all | bytes 262144 | tf_op jit(solution)/shard_map/all_to_all | solution.py:510
  49.9 12.1 %denoise_step.4 = (f32[16,128]{1,0:T(8,128)S(1)}, bf16[16,32,128]{2,1,0:T(8,128)(2,1)S(1)}) custom-call(s32[8]{0:T(128)S(1)} %copy-done, bf16[16,32,128]{2,1,0:T(8,128)(2,1)S(1)} %all_to_all.16.pieces_ref, f32[16,128]{1,0:T(8,128)S(1)} %get-tuple-element.47.lat_ref, bf16[1,8,160,768]{3,2,1,0:T(8,128)(2,1)S(1)} %get-tuple-element.29.refs_0_, ...), custom_call_target="tpu_custom_call" | custom-call | tf_op jit(solution)/shard_map/denoise_step/pallas_call | solution.py:456
  62.0 10.5 %all_to_all.17.pieces_ref = bf16[16,32,128]{2,1,0:T(8,128)(2,1)S(1)} all-to-all(bf16[16,32,128]{2,1,0:T(8,128)(2,1)S(1)} %get-tuple-element.48), channel_id=1, replica_groups=mesh['clip'=2,'tm'=2,'space'=8] {'space','tm'}, dimensions={0} | all-to-all | bytes 262144 | tf_op jit(solution)/shard_map/all_to_all | solution.py:510
  72.5 11.6 %denoise_step.5 = (f32[2,8,16,16]{3,2,1,0:T(8,128)S(1)}, f32[2,8,16,16]{3,2,1,0:T(8,128)S(1)}) custom-call(s32[8]{0:T(128)S(1)} %copy-done, bf16[16,32,128]{2,1,0:T(8,128)(2,1)S(1)} %all_to_all.17.pieces_ref, f32[16,128]{1,0:T(8,128)S(1)} %get-tuple-element.49.lat_ref, bf16[1,8,160,768]{3,2,1,0:T(8,128)(2,1)S(1)} %get-tuple-element.29.refs_0_, ...), custom_call_target="tpu_custom_call" | custom-call | tf_op jit(solution)/shard_map/denoise_step/pallas_call | solution.py:456
  84.2 0.1 collective-permute-start
  84.3 1.3 %collective-permute-done = f32[2,8,16,16]{3,2,1,0:T(8,128)S(1)} collective-permute-done((f32[2,8,16,16]{3,2,1,0:T(8,128)S(1)}, f32[2,8,16,16]{3,2,1,0:T(8,128)S(1)}, u32[]{:S(2)}, u32[]{:S(2)}) %collective-permute-start) | collective-permute-done | bytes 16416 | tf_op jit(solution)/shard_map/ppermute | solution.py:519
  85.6 0.7 slice_add_fusion
Async XLA Ops:
  0.6 0.7 copy-start
  84.2 1.4 %collective-permute-start = (f32[2,8,16,16]{3,2,1,0:T(8,128)S(1)}, f32[2,8,16,16]{3,2,1,0:T(8,128)S(1)}, u32[]{:S(2)}, u32[]{:S(2)}) collective-permute-start(f32[2,8,16,16]{3,2,1,0:T(8,128)S(1)} %get-tuple-element.51), channel_id=1, source_target_pairs={{0,8},{8,0},{1,9},{9,1},{2,10},{10,2},{3,11},{11,3},{4,12},{12,4},... | collective-permute-start | bytes 49160 | tf_op jit(solution)/shard_map/ppermute | solution.py:519

commit v2 on v1

v2 whole, which is shorter than its diff:
```python
import functools
import math

import jax
import jax.numpy as jnp
import numpy as np
from jax import lax
from jax.experimental import pallas as pl
from jax.experimental.pallas import tpu as pltpu
from jax.sharding import PartitionSpec as P

D = 1152
HEADS = 8
HD = 72
INNER = HEADS * HD
CH = 16
FRAMES = 2
STEPS = 3
LEVELS = 16

LANES = 128
WIDE = -(-INNER // LANES) * LANES
PIECE = 32
PACK = LANES // PIECE
PLAN = LANES + PIECE

GRANT = 26 * 1024 * 1024

epsilon = 1e-06
f32 = jnp.float32
bf16 = jnp.bfloat16


def dot(a, b):
    return lax.dot_general(a, b, (((1,), (0,)), ((), ())), preferred_element_type=f32)


def dot_nt(a, b):
    return lax.dot_general(a, b, (((1,), (1,)), ((), ())), preferred_element_type=f32)


def split(x):
    high = x.astype(bf16)
    return high, (x - high.astype(f32)).astype(bf16)


def sincos(count, width):
    half = width // 2
    rates = np.exp(-np.log(10000.0) * np.arange(half) / half)
    angles = np.arange(count)[:, None] * rates[None, :]
    return np.concatenate([np.sin(angles), np.cos(angles)], axis=-1)


def head_masks():
    shape = (HEADS, 1, WIDE)
    head = lax.broadcasted_iota(jnp.int32, shape, 0)
    position = lax.broadcasted_iota(jnp.int32, shape, 2)
    return ((position >= head * HD) & (position < (head + 1) * HD)).astype(f32)


def normalized(values):
    centered = values - jnp.mean(values, axis=-1, keepdims=True)
    return centered * lax.rsqrt(jnp.mean(centered * centered, axis=-1, keepdims=True) + epsilon)


def modulated(values, shift, scale):
    slots = shift.shape[0]
    out = values.reshape(slots, -1, D) * (1.0 + scale)[:, None, :] + shift[:, None, :]
    return out.reshape(values.shape)


def own_hidden(lat, embed, pos_own):
    lanes = lat.shape[1]
    lat_high, lat_low = split(lat)
    lat_high = lat_high.astype(f32)
    zeros = jnp.zeros((LANES - 3 * CH, lanes), f32)
    rows = jnp.concatenate([lat_high, lat_low.astype(f32), lat_high, zeros], axis=0).T.astype(bf16)
    embed_high, embed_low = split(embed)
    weights = jnp.concatenate(
        [embed_high, embed_high, embed_low, jnp.zeros((LANES - 3 * CH, D), bf16)], axis=0
    )
    own = pos_own.shape[0]
    return (dot(rows, weights).reshape(lanes // own, own, D) + pos_own[None]).reshape(lanes, D)


def make_piece(lat, hidden):
    lanes = lat.shape[1]
    centered = hidden - jnp.mean(hidden, axis=-1, keepdims=True)
    scale = lax.rsqrt(jnp.mean(centered * centered, axis=-1, keepdims=True) + epsilon)
    scale = jnp.broadcast_to(scale, (lanes, LANES)).T[:1].astype(bf16).astype(f32)
    scaled = lat * scale
    high = scaled.astype(bf16).astype(f32)
    zeros = jnp.zeros((PIECE // 2 - 3, lanes), f32)
    return jnp.concatenate([high, jnp.ones((2, lanes), f32), scale, zeros], axis=0), scaled - high


def pick(values, low, frames):
    own = LANES // 2 // frames
    lane = lax.broadcasted_iota(jnp.int32, (1, LANES), 1)
    values = jnp.where(low, values, pltpu.roll(values, LANES - own, 1))
    out = jnp.where(lane // own == 0, values, 0.0)
    for g in range(1, frames):
        out = out + jnp.where(lane // own == g, pltpu.roll(values, LANES - g * own, 1), 0.0)
    return out


def placed(block, start):
    rows, width = block.shape
    wide = jnp.concatenate([block, jnp.zeros((rows, LANES - width), f32)], axis=1)
    return pltpu.roll(wide, start, 1) if start else wide


HELD = 16
COPIED = 8


def start_all(copies):
    for copy in copies:
        copy.start()


def build_plans(mods_ref, pos_ref, embed_ref, weight_ref, left_ref, key_plan_ref, value_plan_ref):
    blocks, slots = key_plan_ref.shape[:2]
    tokens = LANES
    embed = embed_ref[...]
    embed = embed - jnp.mean(embed, axis=-1, keepdims=True)
    row = lax.broadcasted_iota(jnp.int32, (PIECE - CH, 1), 0)
    part = lax.broadcasted_iota(jnp.int32, (PIECE, 1), 0)
    for b in range(blocks):
        pos = pos_ref[b * tokens : (b + 1) * tokens]
        pos = pos - jnp.mean(pos, axis=-1, keepdims=True)
        for q in range(slots):
            scale = 1.0 + mods_ref[q, 1:2]
            shift_rows = jnp.where(row < 2, mods_ref[q, 0:1], 0.0)
            left_ref[q * PLAN : (q + 1) * PLAN] = jnp.concatenate(
                [pos * scale, embed * scale, shift_rows], axis=0
            ).astype(bf16)
        for ref, weight in ((key_plan_ref, weight_ref[:INNER]), (value_plan_ref, weight_ref[INNER:])):
            product = dot_nt(left_ref[...], weight)
            for q in range(slots):
                rows = product[q * PLAN : (q + 1) * PLAN]
                group = rows[tokens:]
                group = jnp.where(part == CH + 1, group - group.astype(bf16).astype(f32), group).astype(bf16)
                copies = (ref.shape[2] - tokens) // PIECE
                rows = jnp.concatenate([rows[:tokens].astype(bf16)] + [group] * copies, axis=0)
                if ref.shape[3] > INNER:
                    rows = jnp.concatenate([rows, jnp.zeros((rows.shape[0], ref.shape[3] - INNER), bf16)], axis=1)
                ref[b, q] = rows


def gain_products(gains):
    products = jnp.concatenate(
        [gains[0:1] * gains[1:2], gains[2:3] * gains[3:4], jnp.zeros((6, HD), f32)], axis=0
    ) / math.sqrt(HD)
    place = lax.broadcasted_iota(jnp.int32, (HD, WIDE), 1)
    feature = lax.broadcasted_iota(jnp.int32, (HD, WIDE), 0)
    spread = ((place < INNER) & (lax.rem(place, HD) == feature)).astype(f32)
    return lax.dot_general(
        products, spread, (((1,), (0,)), ((), ())), preferred_element_type=f32, precision=lax.Precision.HIGHEST
    )


def head_normed(values, same_head, gain):
    values = values.astype(bf16).astype(f32)
    total = dot((values * values).astype(bf16), same_head)
    return values * lax.rsqrt(total * (1.0 / HD) + epsilon) * gain


def partner_latents(piece, frames, low):
    lane = lax.broadcasted_iota(jnp.int32, (1, LANES), 1)
    chosen = pick(piece[: PIECE - CH // 2], low, frames)
    rest = piece[PIECE - CH // 2 :]
    rest = jnp.concatenate([rest, pltpu.roll(rest, LANES // 2, 1)], axis=0)
    lat = (chosen[:CH] + rest) / chosen[CH + 2 : CH + 3]
    lat = jnp.where(lane < LANES // 2, lat, 0.0)
    return jnp.where(low, pltpu.roll(lat, LANES // 2, 1), lat)


def prepare_kernel(levels_ref, queue_hbm, pos_hbm, table_hbm, gains_hbm, final_hbm, wsi_hbm, *refs):
    sources, held = refs[:COPIED], refs[COPIED : COPIED + HELD]
    piece_ref, lat_ref, queue_ref, pos_ref, pos_shard_ref, gains_ref, turned_ref, weight_ref, left_ref, sems = refs[
        COPIED + HELD :
    ]
    key_plan_ref, value_plan_ref, mods_ref, gain_rows_ref, rates_ref, final_ref = held[:6]
    pos_own_ref, wsi_ref, _, embed_ref = held[6:10]
    slots = mods_ref.shape[0]
    frames, _, tokens = queue_ref.shape
    own = pos_own_ref.shape[0]
    section, sections = lax.axis_index("tm"), lax.axis_size("tm")
    shard_token = pl.multiple_of(lax.axis_index("space") * tokens, 8)
    own_token = pl.multiple_of(shard_token + section * own, 8)
    stages = [
        [(queue_hbm, queue_ref), (sources[1], embed_ref), (pos_hbm.at[pl.ds(shard_token, tokens)], pos_shard_ref)],
        [(table_hbm.at[levels_ref[q]], mods_ref.at[q]) for q in range(slots)]
        + [(pos_hbm, pos_ref), (wsi_hbm.at[INNER:], weight_ref)],
        [
            (gains_hbm, gains_ref),
            (final_hbm, turned_ref),
            (pos_hbm.at[pl.ds(own_token, own)], pos_own_ref),
            (wsi_hbm.at[:WIDE], wsi_ref),
        ]
        + [pair for pair in zip(sources, held[8:]) if pair[1] is not embed_ref],
    ]
    count = 0
    for i, stage in enumerate(stages):
        stages[i] = [pltpu.make_async_copy(*pair, sems.at[count + j]) for j, pair in enumerate(stage)]
        count += len(stage)
    start_all(stages[0] + stages[1])
    for copy in stages[0]:
        copy.wait()
    lat = placed(queue_ref[0], 0)
    for g in range(1, frames):
        lat = lat + placed(queue_ref[g], g * tokens)
    low = section == 0
    mine = pick(lat, low, frames)
    lat_ref[...] = jnp.where(low, mine, pltpu.roll(mine, LANES // 2, 1))
    piece, rest = make_piece(lat, own_hidden(lat, embed_ref[...], pos_shard_ref[...]))
    rest = pick(rest, section != 0, frames)
    rest = rest[: CH // 2] + pltpu.roll(rest[CH // 2 :], LANES // 2, 1)
    piece = jnp.concatenate([piece[: PIECE - CH // 2], rest], axis=0).astype(bf16)
    for peer in range(piece_ref.shape[0]):
        piece_ref[peer] = piece
    for copy in stages[1]:
        copy.wait()
    start_all(stages[2])
    build_plans(mods_ref, pos_ref, embed_ref, weight_ref, left_ref, key_plan_ref, value_plan_ref)
    for copy in stages[2]:
        copy.wait()
    gain_rows_ref[...] = gain_products(gains_ref[...])
    high, low = split(turned_ref[...])
    final = jnp.concatenate([high.astype(f32), low.astype(f32), jnp.zeros((LANES - 2 * CH, D), f32)], axis=0)
    final_ref[...] = final.T.astype(bf16)
    lanes = lat_ref.shape[1]
    slot = lax.broadcasted_iota(jnp.int32, (1, lanes), 1) // (lanes // slots)
    times = jnp.zeros((1, lanes), f32)
    stride = jnp.zeros((1, lanes), f32)
    before = 0.0
    for q in range(slots):
        time = (levels_ref[q].astype(f32) + 1.0) / LEVELS
        times = jnp.where(slot == q, time, times)
        stride = jnp.where(slot == q, time - before, stride)
        before = time
    rates_ref[...] = jnp.concatenate([times, stride, jnp.zeros((6, lanes), f32)], axis=0)


def step_kernel(pieces_ref, lat_ref, *refs, step):
    first, last = step == 0, step == STEPS - 1
    outs, (cross_ref, mixed_ref, keys_ref, squares_ref) = refs[HELD:-4], refs[-4:]
    (
        key_plan_ref,
        value_plan_ref,
        mods_ref,
        gain_rows_ref,
        rates_ref,
        final_ref,
        pos_own_ref,
        wsi_ref,
        same_head_ref,
        embed_ref,
        head_sum_ref,
        pos_frame_ref,
        noise_ref,
        wso_ref,
        wti_ref,
        wto_ref,
    ) = refs[:HELD]
    lanes = lat_ref.shape[1]
    blocks, slots = key_plan_ref.shape[:2]
    frames = slots * FRAMES
    own = lanes // frames
    devices = pieces_ref.shape[0]
    tokens = LANES
    per_block = devices // blocks
    section, sections = lax.axis_index("tm"), lax.axis_size("tm")
    low = section == 0
    mods = [mods_ref[:, row] for row in range(8)]
    same_head = same_head_ref[...]

    lat = lat_ref[...]
    if first:
        partner = lax.axis_index("space") * sections + (sections - 1 - section)
        lat = lat + partner_latents(pieces_ref[partner].astype(f32), frames // sections, low)

    def own_side():
        hidden = own_hidden(lat, embed_ref[...], pos_own_ref[...])
        yield hidden
        normed = normalized(hidden)
        yield None
        normed = modulated(normed, mods[0], mods[1]).astype(bf16)
        yield None
        queries = dot_nt(normed, wsi_ref[...])
        yield None
        yield head_normed(queries, same_head, gain_rows_ref[0:1])

    for group in range(devices // PACK):
        stacked = pieces_ref[group * PACK : (group + 1) * PACK].astype(f32).reshape(LANES, lanes).T
        for part in range(PACK):
            cross_ref[group * PACK + part] = pltpu.roll(stacked, LANES - part * PIECE, 1) if part else stacked

    def turned(b, g):
        if first:
            held, rows = frames // sections, own * sections
            peers = range(b * per_block + g // held, (b + 1) * per_block, sections)
            at = g % held * rows
        else:
            rows, peers, at = own, range(b * per_block, (b + 1) * per_block), g * own
        return [cross_ref[peer, at : at + rows] for peer in peers]

    row = lax.broadcasted_iota(jnp.int32, (tokens, tokens), 0)
    column = lax.broadcasted_iota(jnp.int32, (tokens, tokens), 1)
    diagonal = row == column
    scale_lane = (lax.broadcasted_iota(jnp.int32, (8, LANES), 1) == CH + 2).astype(bf16)
    row = lax.broadcasted_iota(jnp.int32, (LANES, FRAMES * PIECE), 0)
    column = lax.broadcasted_iota(jnp.int32, (LANES, FRAMES * PIECE), 1)
    own_piece = (row // (HEADS * own) == column // PIECE).astype(f32)
    masks = head_masks()
    head_sum = head_sum_ref[...]

    of_frame = [slice(f * tokens, (f + 1) * tokens) for f in range(FRAMES)]
    pairs = [(b, q) for q in range(slots) for b in range(blocks)]
    rows, scales, weights, totals = {}, {}, {}, [0.0] * slots
    steps = own_side()
    hidden = next(steps)
    for b in range(blocks):
        for q in range(slots):
            tiles = [tile for f in range(FRAMES) for tile in turned(b, q * FRAMES + f)]
            rows[b, q] = jnp.concatenate(tiles, axis=0).astype(bf16)
            scales[b, q] = dot_nt(scale_lane, rows[b, q])[:1]
        for q in range(slots):
            marked = [jnp.where(diagonal, scales[b, q][:, at], 0.0).astype(bf16) for at in of_frame]
            left = jnp.concatenate([jnp.concatenate(marked, axis=0), rows[b, q][:, :PIECE]], axis=1)
            keys = dot(left, key_plan_ref[b, q])
            squares_ref[q] = (keys * keys).astype(bf16)
            keys_ref[q] = keys.astype(bf16)
            if b == 0:
                queries = next(steps, None) if q < 4 else queries
        for q in range(slots):
            sums = dot(jnp.concatenate([squares_ref[q, at] for at in of_frame], axis=1), head_sum)
            scores = []
            for f, at in enumerate(of_frame):
                g = q * FRAMES + f
                spread = (queries[g * own : (g + 1) * own][None] * masks).reshape(HEADS * own, WIDE).astype(bf16)
                scores.append(dot_nt(keys_ref[q, at], spread))
            scores = jnp.concatenate(scores, axis=1)
            weights[b, q] = jnp.exp(scores * lax.rsqrt(sums * (1.0 / HD) + epsilon))
            totals[q] = totals[q] + jnp.sum(weights[b, q], axis=0, keepdims=True)
    by_query, groups = {}, {}
    for b, q in pairs:
        by_query[b, q] = (weights[b, q] * (1.0 / totals[q])).T
    for b, q in pairs:
        pieces = jnp.concatenate([rows[b, q][at, :PIECE] for at in of_frame], axis=1)
        groups[b, q] = dot(by_query[b, q].astype(bf16), pieces) * own_piece
    for q in range(slots):
        mixed = 0.0
        for b in range(blocks):
            scaled = by_query[b, q].reshape(FRAMES, HEADS * own, tokens)
            scaled = jnp.concatenate([scaled[f] * scales[b, q][:, at] for f, at in enumerate(of_frame)], axis=0)
            met = jnp.concatenate([scaled.astype(bf16), groups[b, q].astype(bf16)], axis=1)
            mixed = mixed + dot(met, value_plan_ref[b, q])
        for f in range(FRAMES):
            g = q * FRAMES + f
            tiles = []
            for start in range(0, INNER, LANES):
                stop = min(start + LANES, INNER)
                parts = [
                    mixed[(f * HEADS + h) * own : (f * HEADS + h + 1) * own, start:stop] * masks[h, :, start:stop]
                    for h in range(start // HD, -(-stop // HD))
                ]
                tiles.append(functools.reduce(jnp.add, parts))
            mixed_ref[g * own : (g + 1) * own] = jnp.concatenate(tiles, axis=1)
    mixed = mixed_ref[...].astype(bf16)

    branch = dot(mixed, wso_ref[...])
    hidden = (
        hidden.reshape(slots, FRAMES, own, D)
        + mods[2][:, None, None, :] * branch.reshape(slots, FRAMES, own, D)
        + pos_frame_ref[...].reshape(slots, FRAMES, 1, D)
    ).reshape(lanes, D)
    normed = modulated(normalized(hidden), mods[3], mods[4]).astype(bf16)
    queries = dot_nt(normed, wti_ref[:WIDE])
    keys = dot_nt(normed, wti_ref[INNER : INNER + WIDE])
    both = head_normed(jnp.concatenate([queries, keys], axis=0), same_head, 1.0)
    queries = both[:lanes] * gain_rows_ref[1:2]
    keys = both[lanes:].astype(bf16)
    values = dot_nt(normed, wti_ref[2 * INNER :]).astype(bf16)
    row = lax.broadcasted_iota(jnp.int32, (lanes, lanes), 0)
    column = lax.broadcasted_iota(jnp.int32, (lanes, lanes), 1)
    same_token = (lax.rem(row, own) == lax.rem(column, own)).astype(f32)
    windows = [(h * HD // LANES * LANES, -(-(h + 1) * HD // LANES) * LANES) for h in range(HEADS)]
    scores = []
    for h, (start, stop) in enumerate(windows):
        spread = (queries[:, start:stop] * masks[h, :, start:stop]).astype(bf16)
        scores.append(dot_nt(spread, keys[:, start:stop]))
    weights = [jnp.exp(score) * same_token for score in scores]
    scales = [1.0 / jnp.sum(weight, axis=-1, keepdims=True) for weight in weights]
    results = []
    for (start, stop), weight in zip(windows, weights):
        results.append(dot(weight.astype(bf16), values[:, start : min(stop, INNER)]))
    parts = [[] for _ in range(WIDE // LANES)]
    for h, (start, stop) in enumerate(windows):
        stop = min(stop, INNER)
        result = results[h] * scales[h] * masks[h, :, start:stop]
        for tile in range(start // LANES, -(-stop // LANES)):
            parts[tile].append(result[:, tile * LANES - start : min((tile + 1) * LANES, stop) - start])
    mixed = jnp.concatenate([functools.reduce(jnp.add, part).astype(bf16) for part in parts], axis=1)
    branch = dot(mixed, wto_ref[...])
    hidden = hidden + (mods[5][:, None, :] * branch.reshape(slots, FRAMES * own, D)).reshape(lanes, D)
    final = modulated(normalized(hidden), mods[6], mods[7])
    final_high, final_low = split(final)
    products = dot(jnp.concatenate([final_high, final_low], axis=0), final_ref[...])
    by_high, by_low = products[:lanes].T, products[lanes:].T
    velocity = by_high[:CH] + by_high[CH : 2 * CH] + by_low[:CH]

    slot = lax.broadcasted_iota(jnp.int32, (1, lanes), 1) // (FRAMES * own)
    times, stride = rates_ref[0:1], rates_ref[1:2]
    noise = 0.0
    for f in range(FRAMES):
        block = noise_ref[step, f]
        block = jnp.where(low, block[:, :own], block[:, own:])
        noise = noise + placed(block, (frames - FRAMES + f) * own)
    moved = pltpu.roll(lat - stride * velocity, lanes - FRAMES * own, 1)
    moved = jnp.where(slot == slots - 1, noise, moved)
    if not last:
        lat_out, piece_out = outs
        lat_out[...] = moved
        piece = make_piece(moved, own_hidden(moved, embed_ref[...], pos_own_ref[...]))[0].astype(bf16)
        for peer in range(devices):
            piece_out[peer] = piece
    else:
        keep_out, send_out = outs
        held = frames // sections
        for i, result in enumerate((moved, lat - times * velocity)):
            for g in range(held):
                here = [
                    pltpu.roll(result, (lanes - (half * held + g) * own) % lanes, 1)[:, :own] for half in range(2)
                ]
                for out, block in (
                    (keep_out, jnp.where(low, here[0], here[1])),
                    (send_out, jnp.where(low, here[1], here[0])),
                ):
                    zeros = jnp.zeros_like(block)
                    out[i, g] = jnp.concatenate(
                        [jnp.where(low, block, zeros), jnp.where(low, zeros, block)], axis=1
                    )


def per_device(
    queue_latents,
    fresh_noise,
    slot_levels,
    level_table,
    embed_weight,
    spatial_in,
    spatial_out,
    temporal_in,
    temporal_out,
    norm_gains,
    final_weight,
):
    blocks, _, _, tokens = queue_latents.shape
    sections = lax.axis_size("tm")
    shards = lax.axis_size("space")
    axes = ("space", "tm")
    devices = sections * shards
    own = tokens // sections
    slots = blocks * sections
    frames = slots * FRAMES
    lanes = frames * own
    space_tokens = tokens * shards
    token_blocks = space_tokens // LANES
    partner = [(i, sections - 1 - i) for i in range(sections)]

    pos = jnp.asarray(sincos(space_tokens, D).astype(np.float32))
    pos_frame = jnp.asarray(sincos(frames, D).astype(np.float32))
    head = np.where(np.arange(WIDE) < INNER, np.arange(WIDE) // HD, -1)
    same_head = jnp.asarray(((head[:, None] == head[None, :]) & (head >= 0)[None, :]).astype(np.float32), bf16)
    lane = np.arange(LANES)
    lane_head = lane // own % HEADS
    lane_frame = lane // (HEADS * own)
    head_sum = np.concatenate(
        [(head[:, None] == lane_head[None, :]) & (lane_frame == f)[None, :] for f in range(FRAMES)], axis=0
    )
    head_sum = jnp.asarray(head_sum.astype(np.float32), bf16)

    final_turned = jnp.transpose(final_weight)
    spatial_turned = jnp.transpose(spatial_in)
    temporal_turned = jnp.transpose(temporal_in)

    vmem = pl.BlockSpec(memory_space=pltpu.VMEM)
    smem = pl.BlockSpec(memory_space=pltpu.SMEM)
    hbm = pl.BlockSpec(memory_space=pltpu.HBM)
    dma = pltpu.SemaphoreType.DMA

    def call(kernel, out_shape, arguments, scratch, name):
        spaces = {id(vmem): pltpu.VMEM, id(hbm): pltpu.HBM, id(smem): pltpu.HBM}
        values = [
            pltpu.with_memory_space_constraint(value, spaces[id(spec)]) if id(spec) in spaces else value
            for value, spec in arguments
        ]
        return pl.pallas_call(
            kernel,
            out_shape=out_shape,
            in_specs=[spec for _, spec in arguments],
            out_specs=[vmem] * len(out_shape),
            scratch_shapes=scratch,
            compiler_params=pltpu.CompilerParams(vmem_limit_bytes=GRANT),
            name=name,
        )(*values)

    flat = pltpu.VMEM((CH, lanes), f32)
    piece_shape = pltpu.VMEM((devices, PIECE, lanes), bf16)
    queue = queue_latents.reshape(blocks * FRAMES, CH, tokens)
    copied = [
        same_head,
        embed_weight,
        head_sum,
        pos_frame,
        fresh_noise,
        spatial_out,
        temporal_turned,
        temporal_out,
    ]
    held = [
        pltpu.VMEM((token_blocks, slots, PLAN, WIDE), bf16),
        pltpu.VMEM((token_blocks, slots, LANES + FRAMES * PIECE, INNER), bf16),
        pltpu.VMEM((slots, 8, D), f32),
        pltpu.VMEM((8, WIDE), f32),
        pltpu.VMEM((8, lanes), f32),
        pltpu.VMEM((D, LANES), bf16),
        pltpu.VMEM((own, D), f32),
        pltpu.VMEM((WIDE, D), bf16),
        *(pltpu.VMEM(x.shape, x.dtype) for x in copied),
    ]
    *held, pieces, lat = call(
        prepare_kernel,
        held + [piece_shape, flat],
        [(slot_levels, smem)]
        + [(x, hbm) for x in (queue, pos, level_table, norm_gains, final_turned, spatial_turned, *copied)],
        [
            pltpu.VMEM(queue.shape, f32),
            pltpu.VMEM((space_tokens, D), f32),
            pltpu.VMEM((tokens, D), f32),
            pltpu.VMEM((4, HD), f32),
            pltpu.VMEM((CH, D), f32),
            pltpu.VMEM((2 * INNER, D), bf16),
            pltpu.VMEM((slots * PLAN, D), bf16),
            dma((3 + slots + 2 + 4 + COPIED,)),
        ],
        "slot_plan",
    )
    result_shape = pltpu.VMEM((2, blocks * FRAMES, CH, tokens), f32)
    for step in range(STEPS):
        last = step == STEPS - 1
        gathered = lax.all_to_all(pieces, axes, split_axis=0, concat_axis=0, tiled=True)
        lat, pieces = call(
            functools.partial(step_kernel, step=step),
            [result_shape] * 2 if last else [flat, piece_shape],
            [(x, vmem) for x in (gathered, lat, *held)],
            [pltpu.VMEM((devices, lanes, LANES), f32), pltpu.VMEM((lanes, INNER), f32)]
            + [pltpu.VMEM((slots, FRAMES * LANES, WIDE), bf16)] * 2,
            "denoise_step",
        )

    received = lax.ppermute(pieces, "tm", partner)
    return tuple((lat[i] + received[i]).reshape(queue_latents.shape) for i in range(2))


def solution(mesh):
    return jax.shard_map(
        per_device,
        mesh=mesh,
        in_specs=(
            P(("clip", "tm"), None, None, "space"),
            P("clip", None, None, "space"),
            P("clip"),
            P(),
            P(),
            P(),
            P(),
            P(),
            P(),
            P(),
            P(),
        ),
        out_specs=(P(("clip", "tm"), None, None, "space"), P(("clip", "tm"), None, None, "space")),
        check_vma=False,
    )
```

time: 86.5 us -> 74 us (0.86)
  Pallas kernels: 46.7 us -> 34.8 us
    pallas_call x4, Pallas kernels: 46.7 us -> 34.8 us  [call(): pl.pallas_call(kernel, out_shape=out_shape, in_specs=[spec for _, spec in...]
where the time goes in v2:
time: 74 us; the launch traced here: 73.7 us
  blocking collectives  36.2 us (49%)
  Pallas kernels  34.8 us (47%)
  waiting for transfers between devices  1.33 us (2%)
    all_to_all x3, blocking collectives, per_device(): lax.all_to_all(pieces, axes, split_axis=0, concat_axis=0, tiled=True)  36.2 us
    pallas_call x4, Pallas kernels, call(): pl.pallas_call(kernel, out_shape=out_shape, in_specs=[spec for _, spec in...  34.8 us
  transfers between devices with their start and end apart: 1, of which 1 were waited for; matrix products, arithmetic and copies ran while one was open for 0% of the time, Pallas kernels for 0%

profile of v2, /device:TPU:0, one launch (start us, length us, event | category | flops | bytes accessed | tf_op | source)
XLA Modules:
  0.0 73.7 jit_solution(4377441970925736694)
XLA Ops:
  0.6 10.5 %slot_plan.1 = (bf16[1,8,160,640]{3,2,1,0:T(8,128)(2,1)S(1)}, bf16[1,8,192,576]{3,2,1,0:T(8,128)(2,1)S(1)}, f32[8,8,1152]{2,1,0:T(8,128)S(1)}, f32[8,640]{1,0:T(...) custom-call(s32[8]{0:T(128)} %levels_ref.1, ...), custom_call_target="tpu_custom_call" | custom-call | tf_op jit(solution)/shard_map/slot_plan/pallas_call | solution.py:500
  11.2 15.1 %all_to_all.15.pieces_ref = bf16[16,32,128]{2,1,0:T(8,128)(2,1)S(1)} all-to-all(bf16[16,32,128]{2,1,0:T(8,128)(2,1)S(1)} %get-tuple-element.26), channel_id=1, replica_groups=mesh['clip'=2,'tm'=2,'space'=8] {'space','tm'}, dimensions={0} | all-to-all | bytes 262144 | tf_op jit(solution)/shard_map/all_to_all | solution.py:554
  26.3 8.4 %denoise_step.3 = (f32[16,128]{1,0:T(8,128)S(1)}, bf16[16,32,128]{2,1,0:T(8,128)(2,1)S(1)}) custom-call(bf16[16,32,128]{2,1,0:T(8,128)(2,1)S(1)} %all_to_all.15.pieces_ref, f32[16,128]{1,0:T(8,128)S(1)} %get-tuple-element.27.lat_ref, bf16[1,8,160,640]{3,2,1,0:T(8,128)(2,1)S(1)} %get-tuple-element.28.refs_0_, ...), custom_call_target="tpu_custom_call" | custom-call | tf_op jit(solution)/shard_map/denoise_step/pallas_call | solution.py:500
  34.7 10.5 %all_to_all.16.pieces_ref = bf16[16,32,128]{2,1,0:T(8,128)(2,1)S(1)} all-to-all(bf16[16,32,128]{2,1,0:T(8,128)(2,1)S(1)} %get-tuple-element.44), channel_id=1, replica_groups=mesh['clip'=2,'tm'=2,'space'=8] {'space','tm'}, dimensions={0} | all-to-all | bytes 262144 | tf_op jit(solution)/shard_map/all_to_all | solution.py:554
  45.3 8.1 %denoise_step.4 = (f32[16,128]{1,0:T(8,128)S(1)}, bf16[16,32,128]{2,1,0:T(8,128)(2,1)S(1)}) custom-call(bf16[16,32,128]{2,1,0:T(8,128)(2,1)S(1)} %all_to_all.16.pieces_ref, f32[16,128]{1,0:T(8,128)S(1)} %get-tuple-element.45.lat_ref, bf16[1,8,160,640]{3,2,1,0:T(8,128)(2,1)S(1)} %get-tuple-element.28.refs_0_, ...), custom_call_target="tpu_custom_call" | custom-call | tf_op jit(solution)/shard_map/denoise_step/pallas_call | solution.py:500
  53.3 10.5 %all_to_all.17.pieces_ref = bf16[16,32,128]{2,1,0:T(8,128)(2,1)S(1)} all-to-all(bf16[16,32,128]{2,1,0:T(8,128)(2,1)S(1)} %get-tuple-element.46), channel_id=1, replica_groups=mesh['clip'=2,'tm'=2,'space'=8] {'space','tm'}, dimensions={0} | all-to-all | bytes 262144 | tf_op jit(solution)/shard_map/all_to_all | solution.py:554
  63.9 7.8 %denoise_step.5 = (f32[2,8,16,16]{3,2,1,0:T(8,128)S(1)}, f32[2,8,16,16]{3,2,1,0:T(8,128)S(1)}) custom-call(bf16[16,32,128]{2,1,0:T(8,128)(2,1)S(1)} %all_to_all.17.pieces_ref, f32[16,128]{1,0:T(8,128)S(1)} %get-tuple-element.47.lat_ref, bf16[1,8,160,640]{3,2,1,0:T(8,128)(2,1)S(1)} %get-tuple-element.28.refs_0_, ...), custom_call_target="tpu_custom_call" | custom-call | tf_op jit(solution)/shard_map/denoise_step/pallas_call | solution.py:500
  71.6 0.1 collective-permute-start
  71.7 1.3 %collective-permute-done = f32[2,8,16,16]{3,2,1,0:T(8,128)S(1)} collective-permute-done((f32[2,8,16,16]{3,2,1,0:T(8,128)S(1)}, f32[2,8,16,16]{3,2,1,0:T(8,128)S(1)}, u32[]{:S(2)}, u32[]{:S(2)}) %collective-permute-start) | collective-permute-done | bytes 16416 | tf_op jit(solution)/shard_map/ppermute | solution.py:564
  73.1 0.7 slice_add_fusion
Async XLA Ops:
  71.6 1.4 %collective-permute-start = (f32[2,8,16,16]{3,2,1,0:T(8,128)S(1)}, f32[2,8,16,16]{3,2,1,0:T(8,128)S(1)}, u32[]{:S(2)}, u32[]{:S(2)}) collective-permute-start(f32[2,8,16,16]{3,2,1,0:T(8,128)S(1)} %get-tuple-element.49), channel_id=1, source_target_pairs={{0,8},{8,0},{1,9},{9,1},{2,10},{10,2},{3,11},{11,3},{4,12},{12,4},... | collective-permute-start | bytes 49160 | tf_op jit(solution)/shard_map/ppermute | solution.py:564

commit v3 on v2

--- a/solution.py
+++ b/solution.py
@@ -21,6 +21,7 @@
 LANES = 128
 WIDE = -(-INNER // LANES) * LANES
 PIECE = 32
+SHORT = PIECE - CH // 2
 PACK = LANES // PIECE
 PLAN = LANES + PIECE
 
@@ -90,7 +91,7 @@
     scale = jnp.broadcast_to(scale, (lanes, LANES)).T[:1].astype(bf16).astype(f32)
     scaled = lat * scale
     high = scaled.astype(bf16).astype(f32)
-    zeros = jnp.zeros((PIECE // 2 - 3, lanes), f32)
+    zeros = jnp.zeros((SHORT - CH - 3, lanes), f32)
     return jnp.concatenate([high, jnp.ones((2, lanes), f32), scale, zeros], axis=0), scaled - high
 
 
@@ -110,8 +111,9 @@
     return pltpu.roll(wide, start, 1) if start else wide
 
 
-HELD = 16
-COPIED = 8
+HELD = 13
+COPIED = 5
+LATER = 3
 
 
 def start_all(copies):
@@ -168,17 +170,17 @@
 
 def partner_latents(piece, frames, low):
     lane = lax.broadcasted_iota(jnp.int32, (1, LANES), 1)
-    chosen = pick(piece[: PIECE - CH // 2], low, frames)
-    rest = piece[PIECE - CH // 2 :]
+    chosen = pick(piece[:SHORT], low, frames)
+    rest = piece[SHORT:]
     rest = jnp.concatenate([rest, pltpu.roll(rest, LANES // 2, 1)], axis=0)
     lat = (chosen[:CH] + rest) / chosen[CH + 2 : CH + 3]
     lat = jnp.where(lane < LANES // 2, lat, 0.0)
     return jnp.where(low, pltpu.roll(lat, LANES // 2, 1), lat)
 
 
-def prepare_kernel(levels_ref, queue_hbm, pos_hbm, table_hbm, gains_hbm, final_hbm, wsi_hbm, *refs):
+def prepare_kernel(levels_hbm, queue_hbm, pos_hbm, table_hbm, gains_hbm, final_hbm, wsi_hbm, *refs):
     sources, held = refs[:COPIED], refs[COPIED : COPIED + HELD]
-    piece_ref, lat_ref, queue_ref, pos_ref, pos_shard_ref, gains_ref, turned_ref, weight_ref, left_ref, sems = refs[
+    piece_ref, lat_ref, levels_ref, table_ref, queue_ref, pos_ref, pos_shard_ref, gains_ref, turned_ref, weight_ref, left_ref, sems = refs[
         COPIED + HELD :
     ]
     key_plan_ref, value_plan_ref, mods_ref, gain_rows_ref, rates_ref, final_ref = held[:6]
@@ -190,12 +192,16 @@
     shard_token = pl.multiple_of(lax.axis_index("space") * tokens, 8)
     own_token = pl.multiple_of(shard_token + section * own, 8)
     stages = [
-        [(queue_hbm, queue_ref), (sources[1], embed_ref), (pos_hbm.at[pl.ds(shard_token, tokens)], pos_shard_ref)],
-        [(table_hbm.at[levels_ref[q]], mods_ref.at[q]) for q in range(slots)]
-        + [(pos_hbm, pos_ref), (wsi_hbm.at[INNER:], weight_ref)],
         [
+            (levels_hbm, levels_ref),
+            (queue_hbm, queue_ref),
+            (sources[1], embed_ref),
+            (pos_hbm.at[pl.ds(shard_token, tokens)], pos_shard_ref),
             (gains_hbm, gains_ref),
             (final_hbm, turned_ref),
+        ],
+        [(table_hbm, table_ref), (pos_hbm, pos_ref), (wsi_hbm.at[INNER:], weight_ref)],
+        [
             (pos_hbm.at[pl.ds(own_token, own)], pos_own_ref),
             (wsi_hbm.at[:WIDE], wsi_ref),
         ]
@@ -205,7 +211,8 @@
     for i, stage in enumerate(stages):
         stages[i] = [pltpu.make_async_copy(*pair, sems.at[count + j]) for j, pair in enumerate(stage)]
         count += len(stage)
-    start_all(stages[0] + stages[1])
+    for stage in stages:
+        start_all(stage)
     for copy in stages[0]:
         copy.wait()
     lat = placed(queue_ref[0], 0)
@@ -217,15 +224,9 @@
     piece, rest = make_piece(lat, own_hidden(lat, embed_ref[...], pos_shard_ref[...]))
     rest = pick(rest, section != 0, frames)
     rest = rest[: CH // 2] + pltpu.roll(rest[CH // 2 :], LANES // 2, 1)
-    piece = jnp.concatenate([piece[: PIECE - CH // 2], rest], axis=0).astype(bf16)
+    piece = jnp.concatenate([piece, rest], axis=0).astype(bf16)
     for peer in range(piece_ref.shape[0]):
         piece_ref[peer] = piece
-    for copy in stages[1]:
-        copy.wait()
-    start_all(stages[2])
-    build_plans(mods_ref, pos_ref, embed_ref, weight_ref, left_ref, key_plan_ref, value_plan_ref)
-    for copy in stages[2]:
-        copy.wait()
     gain_rows_ref[...] = gain_products(gains_ref[...])
     high, low = split(turned_ref[...])
     final = jnp.concatenate([high.astype(f32), low.astype(f32), jnp.zeros((LANES - 2 * CH, D), f32)], axis=0)
@@ -241,11 +242,26 @@
         stride = jnp.where(slot == q, time - before, stride)
         before = time
     rates_ref[...] = jnp.concatenate([times, stride, jnp.zeros((6, lanes), f32)], axis=0)
+    for copy in stages[1]:
+        copy.wait()
+    for q in range(slots):
+        mods_ref[q] = table_ref[levels_ref[q]]
+    build_plans(mods_ref, pos_ref, embed_ref, weight_ref, left_ref, key_plan_ref, value_plan_ref)
+    for copy in stages[2]:
+        copy.wait()
 
 
 def step_kernel(pieces_ref, lat_ref, *refs, step):
     first, last = step == 0, step == STEPS - 1
-    outs, (cross_ref, mixed_ref, keys_ref, squares_ref) = refs[HELD:-4], refs[-4:]
+    held, later, refs = refs[:HELD], refs[HELD : HELD + LATER], refs[HELD + LATER :]
+    outs, refs = refs[:2], refs[2:]
+    copies = []
+    if first:
+        later_hbm, later, refs = later, refs[:LATER], refs[LATER:]
+        copies = [pltpu.make_async_copy(*pair, refs[-1].at[i]) for i, pair in enumerate(zip(later_hbm, later))]
+        start_all(copies)
+    cross_ref, mixed_ref, keys_ref, squares_ref = refs[:4]
+    wso_ref, wti_ref, wto_ref = later
     (
         key_plan_ref,
         value_plan_ref,
@@ -260,10 +276,7 @@
         head_sum_ref,
         pos_frame_ref,
         noise_ref,
-        wso_ref,
-        wti_ref,
-        wto_ref,
-    ) = refs[:HELD]
+    ) = held
     lanes = lat_ref.shape[1]
     blocks, slots = key_plan_ref.shape[:2]
     frames = slots * FRAMES
@@ -293,7 +306,10 @@
         yield head_normed(queries, same_head, gain_rows_ref[0:1])
 
     for group in range(devices // PACK):
-        stacked = pieces_ref[group * PACK : (group + 1) * PACK].astype(f32).reshape(LANES, lanes).T
+        stacked = pieces_ref[group * PACK : (group + 1) * PACK].astype(f32)
+        if not first:
+            stacked = jnp.concatenate([stacked, jnp.zeros((PACK, PIECE - SHORT, lanes), f32)], axis=1)
+        stacked = stacked.reshape(LANES, lanes).T
         for part in range(PACK):
             cross_ref[group * PACK + part] = pltpu.roll(stacked, LANES - part * PIECE, 1) if part else stacked
 
@@ -370,6 +386,8 @@
             mixed_ref[g * own : (g + 1) * own] = jnp.concatenate(tiles, axis=1)
     mixed = mixed_ref[...].astype(bf16)
 
+    for copy in copies:
+        copy.wait()
     branch = dot(mixed, wso_ref[...])
     hidden = (
         hidden.reshape(slots, FRAMES, own, D)
@@ -487,16 +505,12 @@
     temporal_turned = jnp.transpose(temporal_in)
 
     vmem = pl.BlockSpec(memory_space=pltpu.VMEM)
-    smem = pl.BlockSpec(memory_space=pltpu.SMEM)
     hbm = pl.BlockSpec(memory_space=pltpu.HBM)
     dma = pltpu.SemaphoreType.DMA
 
     def call(kernel, out_shape, arguments, scratch, name):
-        spaces = {id(vmem): pltpu.VMEM, id(hbm): pltpu.HBM, id(smem): pltpu.HBM}
-        values = [
-            pltpu.with_memory_space_constraint(value, spaces[id(spec)]) if id(spec) in spaces else value
-            for value, spec in arguments
-        ]
+        spaces = {id(vmem): pltpu.VMEM, id(hbm): pltpu.HBM}
+        values = [pltpu.with_memory_space_constraint(value, spaces[id(spec)]) for value, spec in arguments]
         return pl.pallas_call(
             kernel,
             out_shape=out_shape,
@@ -508,7 +522,8 @@
         )(*values)
 
     flat = pltpu.VMEM((CH, lanes), f32)
-    piece_shape = pltpu.VMEM((devices, PIECE, lanes), bf16)
+    first_piece_shape = pltpu.VMEM((devices, PIECE, lanes), bf16)
+    piece_shape = pltpu.VMEM((devices, SHORT, lanes), bf16)
     queue = queue_latents.reshape(blocks * FRAMES, CH, tokens)
     copied = [
         same_head,
@@ -516,10 +531,8 @@
         head_sum,
         pos_frame,
         fresh_noise,
-        spatial_out,
-        temporal_turned,
-        temporal_out,
     ]
+    later = [spatial_out, temporal_turned, temporal_out]
     held = [
         pltpu.VMEM((token_blocks, slots, PLAN, WIDE), bf16),
         pltpu.VMEM((token_blocks, slots, LANES + FRAMES * PIECE, INNER), bf16),
@@ -533,10 +546,11 @@
     ]
     *held, pieces, lat = call(
         prepare_kernel,
-        held + [piece_shape, flat],
-        [(slot_levels, smem)]
-        + [(x, hbm) for x in (queue, pos, level_table, norm_gains, final_turned, spatial_turned, *copied)],
+        held + [first_piece_shape, flat],
+        [(x, hbm) for x in (slot_levels, queue, pos, level_table, norm_gains, final_turned, spatial_turned, *copied)],
         [
+            pltpu.SMEM((slots,), jnp.int32),
+            pltpu.VMEM(level_table.shape, f32),
             pltpu.VMEM(queue.shape, f32),
             pltpu.VMEM((space_tokens, D), f32),
             pltpu.VMEM((tokens, D), f32),
@@ -544,7 +558,7 @@
             pltpu.VMEM((CH, D), f32),
             pltpu.VMEM((2 * INNER, D), bf16),
             pltpu.VMEM((slots * PLAN, D), bf16),
-            dma((3 + slots + 2 + 4 + COPIED,)),
+            dma((11 + COPIED,)),
         ],
         "slot_plan",
     )
@@ -552,14 +566,20 @@
     for step in range(STEPS):
         last = step == STEPS - 1
         gathered = lax.all_to_all(pieces, axes, split_axis=0, concat_axis=0, tiled=True)
-        lat, pieces = call(
+        out_shape = [result_shape] * 2 if last else [flat, piece_shape]
+        scratch = [pltpu.VMEM((devices, lanes, LANES), f32), pltpu.VMEM((lanes, INNER), f32)]
+        scratch += [pltpu.VMEM((slots, FRAMES * LANES, WIDE), bf16)] * 2
+        if step == 0:
+            out_shape += [pltpu.VMEM(x.shape, x.dtype) for x in later]
+            scratch += [dma((LATER,))]
+        lat, pieces, *brought = call(
             functools.partial(step_kernel, step=step),
-            [result_shape] * 2 if last else [flat, piece_shape],
-            [(x, vmem) for x in (gathered, lat, *held)],
-            [pltpu.VMEM((devices, lanes, LANES), f32), pltpu.VMEM((lanes, INNER), f32)]
-            + [pltpu.VMEM((slots, FRAMES * LANES, WIDE), bf16)] * 2,
+            out_shape,
+            [(x, vmem) for x in (gathered, lat, *held)] + [(x, hbm if step == 0 else vmem) for x in later],
+            scratch,
             "denoise_step",
         )
+        later = brought or later
 
     received = lax.ppermute(pieces, "tm", partner)
     return tuple((lat[i] + received[i]).reshape(queue_latents.shape) for i in range(2))

time: 74 us -> 70.8 us (0.957)
  Pallas kernels: 34.8 us -> 32.7 us
  blocking collectives: 36.2 us -> 35.1 us
    pallas_call x4, Pallas kernels: 34.8 us -> 32.7 us  [call(): pl.pallas_call(kernel, out_shape=out_shape, in_specs=[spec for _, spec in...]
    all_to_all x3, blocking collectives: 36.2 us -> 35.1 us  [per_device(): lax.all_to_all(pieces, axes, split_axis=0, concat_axis=0, tiled=True)]
where the time goes in v3:
time: 70.8 us; the launch traced here: 70.5 us
  blocking collectives  35.1 us (50%)
  Pallas kernels  32.7 us (46%)
  waiting for transfers between devices  1.33 us (2%)
    all_to_all x3, blocking collectives, per_device(): lax.all_to_all(pieces, axes, split_axis=0, concat_axis=0, tiled=True)  35.1 us
    pallas_call x4, Pallas kernels, call(): pl.pallas_call(kernel, out_shape=out_shape, in_specs=[spec for _, spec in...  32.7 us
  transfers between devices with their start and end apart: 1, of which 1 were waited for; matrix products, arithmetic and copies ran while one was open for 0% of the time, Pallas kernels for 0%

profile of v3, /device:TPU:0, one launch (start us, length us, event | category | flops | bytes accessed | tf_op | source)
XLA Modules:
  0.0 70.5 jit_solution(9646572229881358300)
XLA Ops:
  0.6 7.7 %slot_plan.1 = (bf16[1,8,160,640]{3,2,1,0:T(8,128)(2,1)S(1)}, bf16[1,8,192,576]{3,2,1,0:T(8,128)(2,1)S(1)}, f32[8,8,1152]{2,1,0:T(8,128)S(1)}, f32[8,640]{1,0:T(...) custom-call(s32[8]{0:T(128)} %levels_hbm.1, ...), custom_call_target="tpu_custom_call" | custom-call | tf_op jit(solution)/shard_map/slot_plan/pallas_call | solution.py:514
  8.4 15.1 %all_to_all.15.pieces_ref = bf16[16,32,128]{2,1,0:T(8,128)(2,1)S(1)} all-to-all(bf16[16,32,128]{2,1,0:T(8,128)(2,1)S(1)} %get-tuple-element.26), channel_id=1, replica_groups=mesh['clip'=2,'tm'=2,'space'=8] {'space','tm'}, dimensions={0} | all-to-all | bytes 262144 | tf_op jit(solution)/shard_map/all_to_all | solution.py:568
  23.5 9.1 %denoise_step.3 = (f32[16,128]{1,0:T(8,128)S(1)}, bf16[16,24,128]{2,1,0:T(8,128)(2,1)S(1)}, bf16[576,1152]{1,0:T(8,128)(2,1)S(1)}, bf16[1728,1152]{1,0:T(8,128)(2,1)S(1)}, bf16[576,1152]{1,0:T(8,128)(2,1)S(1)}) custom-call(bf16[16,32,128]{2,1,0:T(8,128)(2,1)S(1)} %all_to_all.15.pieces_ref, f32[16,128]{1,0:T(8,128)S(1)} %get-tuple-element.27.lat_ref, ...), custom_call_target="tpu_custom_call" | custom-call | tf_op jit(solution)/shard_map/denoise_step/pallas_call | solution.py:514
  32.6 10.0 %all_to_all.16.pieces_ref = bf16[16,24,128]{2,1,0:T(8,128)(2,1)S(1)} all-to-all(bf16[16,24,128]{2,1,0:T(8,128)(2,1)S(1)} %get-tuple-element.41), channel_id=1, replica_groups=mesh['clip'=2,'tm'=2,'space'=8] {'space','tm'}, dimensions={0} | all-to-all | bytes 196608 | tf_op jit(solution)/shard_map/all_to_all | solution.py:568
  42.6 8.1 %denoise_step.4 = (f32[16,128]{1,0:T(8,128)S(1)}, bf16[16,24,128]{2,1,0:T(8,128)(2,1)S(1)}) custom-call(bf16[16,24,128]{2,1,0:T(8,128)(2,1)S(1)} %all_to_all.16.pieces_ref, f32[16,128]{1,0:T(8,128)S(1)} %get-tuple-element.42.lat_ref, bf16[1,8,160,640]{3,2,1,0:T(8,128)(2,1)S(1)} %get-tuple-element.28.refs_0_, ...), custom_call_target="tpu_custom_call" | custom-call | tf_op jit(solution)/shard_map/denoise_step/pallas_call | solution.py:514
  50.7 10.0 %all_to_all.17.pieces_ref = bf16[16,24,128]{2,1,0:T(8,128)(2,1)S(1)} all-to-all(bf16[16,24,128]{2,1,0:T(8,128)(2,1)S(1)} %get-tuple-element.46), channel_id=1, replica_groups=mesh['clip'=2,'tm'=2,'space'=8] {'space','tm'}, dimensions={0} | all-to-all | bytes 196608 | tf_op jit(solution)/shard_map/all_to_all | solution.py:568
  60.7 7.8 %denoise_step.5 = (f32[2,8,16,16]{3,2,1,0:T(8,128)S(1)}, f32[2,8,16,16]{3,2,1,0:T(8,128)S(1)}) custom-call(bf16[16,24,128]{2,1,0:T(8,128)(2,1)S(1)} %all_to_all.17.pieces_ref, f32[16,128]{1,0:T(8,128)S(1)} %get-tuple-element.47.lat_ref, bf16[1,8,160,640]{3,2,1,0:T(8,128)(2,1)S(1)} %get-tuple-element.28.refs_0_, ...), custom_call_target="tpu_custom_call" | custom-call | tf_op jit(solution)/shard_map/denoise_step/pallas_call | solution.py:514
  68.4 0.1 collective-permute-start
  68.5 1.3 %collective-permute-done = f32[2,8,16,16]{3,2,1,0:T(8,128)S(1)} collective-permute-done((f32[2,8,16,16]{3,2,1,0:T(8,128)S(1)}, f32[2,8,16,16]{3,2,1,0:T(8,128)S(1)}, u32[]{:S(2)}, u32[]{:S(2)}) %collective-permute-start) | collective-permute-done | bytes 16416 | tf_op jit(solution)/shard_map/ppermute | solution.py:584
  69.8 0.7 slice_add_fusion
Async XLA Ops:
  68.4 1.4 %collective-permute-start = (f32[2,8,16,16]{3,2,1,0:T(8,128)S(1)}, f32[2,8,16,16]{3,2,1,0:T(8,128)S(1)}, u32[]{:S(2)}, u32[]{:S(2)}) collective-permute-start(f32[2,8,16,16]{3,2,1,0:T(8,128)S(1)} %get-tuple-element.49), channel_id=1, source_target_pairs={{0,8},{8,0},{1,9},{9,1},{2,10},{10,2},{3,11},{11,3},{4,12},{12,4},... | collective-permute-start | bytes 49160 | tf_op jit(solution)/shard_map/ppermute | solution.py:584

commit v4 on v3

--- a/solution.py
+++ b/solution.py
@@ -121,7 +121,7 @@
         copy.start()
 
 
-def build_plans(mods_ref, pos_ref, embed_ref, weight_ref, left_ref, key_plan_ref, value_plan_ref):
+def build_plans(mods_ref, pos_ref, embed_ref, weight_ref, left_ref, key_plan_ref, value_plan_ref, query_ref):
     blocks, slots = key_plan_ref.shape[:2]
     tokens = LANES
     embed = embed_ref[...]
@@ -137,7 +137,7 @@
             left_ref[q * PLAN : (q + 1) * PLAN] = jnp.concatenate(
                 [pos * scale, embed * scale, shift_rows], axis=0
             ).astype(bf16)
-        for ref, weight in ((key_plan_ref, weight_ref[:INNER]), (value_plan_ref, weight_ref[INNER:])):
+        for ref, weight in ((key_plan_ref, weight_ref[INNER : 2 * INNER]), (value_plan_ref, weight_ref[2 * INNER :])):
             product = dot_nt(left_ref[...], weight)
             for q in range(slots):
                 rows = product[q * PLAN : (q + 1) * PLAN]
@@ -148,6 +148,9 @@
                 if ref.shape[3] > INNER:
                     rows = jnp.concatenate([rows, jnp.zeros((rows.shape[0], ref.shape[3] - INNER), bf16)], axis=1)
                 ref[b, q] = rows
+                if b == 0 and ref is key_plan_ref:
+                    for start in range(q * LANES, WIDE, slots * LANES):
+                        query_ref[:, start : start + LANES] = weight_ref[start : start + LANES].T
 
 
 def gain_products(gains):
@@ -200,10 +203,9 @@
             (gains_hbm, gains_ref),
             (final_hbm, turned_ref),
         ],
-        [(table_hbm, table_ref), (pos_hbm, pos_ref), (wsi_hbm.at[INNER:], weight_ref)],
+        [(table_hbm, table_ref), (pos_hbm, pos_ref), (wsi_hbm, weight_ref)],
         [
             (pos_hbm.at[pl.ds(own_token, own)], pos_own_ref),
-            (wsi_hbm.at[:WIDE], wsi_ref),
         ]
         + [pair for pair in zip(sources, held[8:]) if pair[1] is not embed_ref],
     ]
@@ -246,7 +248,7 @@
         copy.wait()
     for q in range(slots):
         mods_ref[q] = table_ref[levels_ref[q]]
-    build_plans(mods_ref, pos_ref, embed_ref, weight_ref, left_ref, key_plan_ref, value_plan_ref)
+    build_plans(mods_ref, pos_ref, embed_ref, weight_ref, left_ref, key_plan_ref, value_plan_ref, wsi_ref)
     for copy in stages[2]:
         copy.wait()
 
@@ -258,7 +260,9 @@
     copies = []
     if first:
         later_hbm, later, refs = later, refs[:LATER], refs[LATER:]
-        copies = [pltpu.make_async_copy(*pair, refs[-1].at[i]) for i, pair in enumerate(zip(later_hbm, later))]
+        wti_raw = refs[-2]
+        targets = (later[0], wti_raw, later[2])
+        copies = [pltpu.make_async_copy(*pair, refs[-1].at[i]) for i, pair in enumerate(zip(later_hbm, targets))]
         start_all(copies)
     cross_ref, mixed_ref, keys_ref, squares_ref = refs[:4]
     wso_ref, wti_ref, wto_ref = later
@@ -301,7 +305,7 @@
         yield None
         normed = modulated(normed, mods[0], mods[1]).astype(bf16)
         yield None
-        queries = dot_nt(normed, wsi_ref[...])
+        queries = dot(normed, wsi_ref[...])
         yield None
         yield head_normed(queries, same_head, gain_rows_ref[0:1])
 
@@ -332,6 +336,12 @@
     masks = head_masks()
     head_sum = head_sum_ref[...]
 
+    turns = []
+    if first:
+        for i, width in enumerate((WIDE, WIDE, INNER)):
+            for start in range(0, width, LANES):
+                stop = min(start + LANES, width)
+                turns.append((slice(i * WIDE + start, i * WIDE + stop), slice(i * INNER + start, i * INNER + stop)))
     of_frame = [slice(f * tokens, (f + 1) * tokens) for f in range(FRAMES)]
     pairs = [(b, q) for q in range(slots) for b in range(blocks)]
     rows, scales, weights, totals = {}, {}, {}, [0.0] * slots
@@ -350,7 +360,13 @@
             keys_ref[q] = keys.astype(bf16)
             if b == 0:
                 queries = next(steps, None) if q < 4 else queries
+        if b == blocks - 1:
+            for copy in copies:
+                copy.wait()
         for q in range(slots):
+            if b == blocks - 1:
+                for to, source in turns[q :: slots]:
+                    wti_ref[:, to] = wti_raw[source].T
             sums = dot(jnp.concatenate([squares_ref[q, at] for at in of_frame], axis=1), head_sum)
             scores = []
             for f, at in enumerate(of_frame):
@@ -386,8 +402,6 @@
             mixed_ref[g * own : (g + 1) * own] = jnp.concatenate(tiles, axis=1)
     mixed = mixed_ref[...].astype(bf16)
 
-    for copy in copies:
-        copy.wait()
     branch = dot(mixed, wso_ref[...])
     hidden = (
         hidden.reshape(slots, FRAMES, own, D)
@@ -395,12 +409,12 @@
         + pos_frame_ref[...].reshape(slots, FRAMES, 1, D)
     ).reshape(lanes, D)
     normed = modulated(normalized(hidden), mods[3], mods[4]).astype(bf16)
-    queries = dot_nt(normed, wti_ref[:WIDE])
-    keys = dot_nt(normed, wti_ref[INNER : INNER + WIDE])
+    projected = dot(normed, wti_ref[...])
+    queries, keys = projected[:, :WIDE], projected[:, WIDE : 2 * WIDE]
+    values = projected[:, 2 * WIDE :].astype(bf16)
     both = head_normed(jnp.concatenate([queries, keys], axis=0), same_head, 1.0)
     queries = both[:lanes] * gain_rows_ref[1:2]
     keys = both[lanes:].astype(bf16)
-    values = dot_nt(normed, wti_ref[2 * INNER :]).astype(bf16)
     row = lax.broadcasted_iota(jnp.int32, (lanes, lanes), 0)
     column = lax.broadcasted_iota(jnp.int32, (lanes, lanes), 1)
     same_token = (lax.rem(row, own) == lax.rem(column, own)).astype(f32)
@@ -541,7 +555,7 @@
         pltpu.VMEM((8, lanes), f32),
         pltpu.VMEM((D, LANES), bf16),
         pltpu.VMEM((own, D), f32),
-        pltpu.VMEM((WIDE, D), bf16),
+        pltpu.VMEM((D, WIDE), bf16),
         *(pltpu.VMEM(x.shape, x.dtype) for x in copied),
     ]
     *held, pieces, lat = call(
@@ -556,7 +570,7 @@
             pltpu.VMEM((tokens, D), f32),
             pltpu.VMEM((4, HD), f32),
             pltpu.VMEM((CH, D), f32),
-            pltpu.VMEM((2 * INNER, D), bf16),
+            pltpu.VMEM((3 * INNER, D), bf16),
             pltpu.VMEM((slots * PLAN, D), bf16),
             dma((11 + COPIED,)),
         ],
@@ -570,8 +584,9 @@
         scratch = [pltpu.VMEM((devices, lanes, LANES), f32), pltpu.VMEM((lanes, INNER), f32)]
         scratch += [pltpu.VMEM((slots, FRAMES * LANES, WIDE), bf16)] * 2
         if step == 0:
-            out_shape += [pltpu.VMEM(x.shape, x.dtype) for x in later]
-            scratch += [dma((LATER,))]
+            later_shapes = (spatial_out.shape, (D, 2 * WIDE + INNER), temporal_out.shape)
+            out_shape += [pltpu.VMEM(shape, bf16) for shape in later_shapes]
+            scratch += [pltpu.VMEM(temporal_turned.shape, bf16), dma((LATER,))]
         lat, pieces, *brought = call(
             functools.partial(step_kernel, step=step),
             out_shape,

time: 70.8 us -> 70.4 us (level)
  no operation moved by 1% of the time
where the time goes in v4:
time: 70.4 us; the launch traced here: 70.1 us
  blocking collectives  35.1 us (50%)
  Pallas kernels  32.2 us (46%)
  waiting for transfers between devices  1.33 us (2%)
    all_to_all x3, blocking collectives, per_device(): lax.all_to_all(pieces, axes, split_axis=0, concat_axis=0, tiled=True)  35.1 us
    pallas_call x4, Pallas kernels, call(): pl.pallas_call(kernel, out_shape=out_shape, in_specs=[spec for _, spec in...  32.2 us
  transfers between devices with their start and end apart: 1, of which 1 were waited for; matrix products, arithmetic and copies ran while one was open for 0% of the time, Pallas kernels for 0%

profile of v4, /device:TPU:0, one launch (start us, length us, event | category | flops | bytes accessed | tf_op | source)
XLA Modules:
  0.0 70.1 jit_solution(12846620350644167180)
XLA Ops:
  0.6 8.1 %slot_plan.1 = (bf16[1,8,160,640]{3,2,1,0:T(8,128)(2,1)S(1)}, bf16[1,8,192,576]{3,2,1,0:T(8,128)(2,1)S(1)}, f32[8,8,1152]{2,1,0:T(8,128)S(1)}, f32[8,640]{1,0:T(...) custom-call(s32[8]{0:T(128)} %levels_hbm.1, ...), custom_call_target="tpu_custom_call" | custom-call | tf_op jit(solution)/shard_map/slot_plan/pallas_call | solution.py:528
  8.8 15.1 %all_to_all.15.pieces_ref = bf16[16,32,128]{2,1,0:T(8,128)(2,1)S(1)} all-to-all(bf16[16,32,128]{2,1,0:T(8,128)(2,1)S(1)} %get-tuple-element.26), channel_id=1, replica_groups=mesh['clip'=2,'tm'=2,'space'=8] {'space','tm'}, dimensions={0} | all-to-all | bytes 262144 | tf_op jit(solution)/shard_map/all_to_all | solution.py:582
  23.9 9.5 %denoise_step.3 = (f32[16,128]{1,0:T(8,128)S(1)}, bf16[16,24,128]{2,1,0:T(8,128)(2,1)S(1)}, bf16[576,1152]{1,0:T(8,128)(2,1)S(1)}, bf16[1152,1856]{1,0:T(8,128)(2,1)S(1)}, bf16[576,1152]{1,0:T(8,128)(2,1)S(1)}) custom-call(bf16[16,32,128]{2,1,0:T(8,128)(2,1)S(1)} %all_to_all.15.pieces_ref, f32[16,128]{1,0:T(8,128)S(1)} %get-tuple-element.27.lat_ref, ...), custom_call_target="tpu_custom_call" | custom-call | tf_op jit(solution)/shard_map/denoise_step/pallas_call | solution.py:528
  33.4 10.0 %all_to_all.16.pieces_ref = bf16[16,24,128]{2,1,0:T(8,128)(2,1)S(1)} all-to-all(bf16[16,24,128]{2,1,0:T(8,128)(2,1)S(1)} %get-tuple-element.41), channel_id=1, replica_groups=mesh['clip'=2,'tm'=2,'space'=8] {'space','tm'}, dimensions={0} | all-to-all | bytes 196608 | tf_op jit(solution)/shard_map/all_to_all | solution.py:582
  43.4 7.5 %denoise_step.4 = (f32[16,128]{1,0:T(8,128)S(1)}, bf16[16,24,128]{2,1,0:T(8,128)(2,1)S(1)}) custom-call(bf16[16,24,128]{2,1,0:T(8,128)(2,1)S(1)} %all_to_all.16.pieces_ref, f32[16,128]{1,0:T(8,128)S(1)} %get-tuple-element.42.lat_ref, bf16[1,8,160,640]{3,2,1,0:T(8,128)(2,1)S(1)} %get-tuple-element.28.refs_0_, ...), custom_call_target="tpu_custom_call" | custom-call | tf_op jit(solution)/shard_map/denoise_step/pallas_call | solution.py:528
  50.9 10.0 %all_to_all.17.pieces_ref = bf16[16,24,128]{2,1,0:T(8,128)(2,1)S(1)} all-to-all(bf16[16,24,128]{2,1,0:T(8,128)(2,1)S(1)} %get-tuple-element.46), channel_id=1, replica_groups=mesh['clip'=2,'tm'=2,'space'=8] {'space','tm'}, dimensions={0} | all-to-all | bytes 196608 | tf_op jit(solution)/shard_map/all_to_all | solution.py:582
  60.9 7.1 %denoise_step.5 = (f32[2,8,16,16]{3,2,1,0:T(8,128)S(1)}, f32[2,8,16,16]{3,2,1,0:T(8,128)S(1)}) custom-call(bf16[16,24,128]{2,1,0:T(8,128)(2,1)S(1)} %all_to_all.17.pieces_ref, f32[16,128]{1,0:T(8,128)S(1)} %get-tuple-element.47.lat_ref, bf16[1,8,160,640]{3,2,1,0:T(8,128)(2,1)S(1)} %get-tuple-element.28.refs_0_, ...), custom_call_target="tpu_custom_call" | custom-call | tf_op jit(solution)/shard_map/denoise_step/pallas_call | solution.py:528
  68.0 0.1 collective-permute-start
  68.1 1.3 %collective-permute-done = f32[2,8,16,16]{3,2,1,0:T(8,128)S(1)} collective-permute-done((f32[2,8,16,16]{3,2,1,0:T(8,128)S(1)}, f32[2,8,16,16]{3,2,1,0:T(8,128)S(1)}, u32[]{:S(2)}, u32[]{:S(2)}) %collective-permute-start) | collective-permute-done | bytes 16416 | tf_op jit(solution)/shard_map/ppermute | solution.py:599
  69.4 0.7 slice_add_fusion
Async XLA Ops:
  68.0 1.4 %collective-permute-start = (f32[2,8,16,16]{3,2,1,0:T(8,128)S(1)}, f32[2,8,16,16]{3,2,1,0:T(8,128)S(1)}, u32[]{:S(2)}, u32[]{:S(2)}) collective-permute-start(f32[2,8,16,16]{3,2,1,0:T(8,128)S(1)} %get-tuple-element.49), channel_id=1, source_target_pairs={{0,8},{8,0},{1,9},{9,1},{2,10},{10,2},{3,11},{11,3},{4,12},{12,4},... | collective-permute-start | bytes 49160 | tf_op jit(solution)/shard_map/ppermute | solution.py:599

commit v5 on v4

--- a/solution.py
+++ b/solution.py
@@ -112,7 +112,7 @@
 
 
 HELD = 13
-COPIED = 5
+COPIED = 8
 LATER = 3
 
 
@@ -182,9 +182,9 @@
 
 
 def prepare_kernel(levels_hbm, queue_hbm, pos_hbm, table_hbm, gains_hbm, final_hbm, wsi_hbm, *refs):
-    sources, held = refs[:COPIED], refs[COPIED : COPIED + HELD]
+    sources, held = refs[:COPIED], refs[COPIED : COPIED + HELD + LATER]
     piece_ref, lat_ref, levels_ref, table_ref, queue_ref, pos_ref, pos_shard_ref, gains_ref, turned_ref, weight_ref, left_ref, sems = refs[
-        COPIED + HELD :
+        COPIED + HELD + LATER :
     ]
     key_plan_ref, value_plan_ref, mods_ref, gain_rows_ref, rates_ref, final_ref = held[:6]
     pos_own_ref, wsi_ref, _, embed_ref = held[6:10]
@@ -257,15 +257,10 @@
     first, last = step == 0, step == STEPS - 1
     held, later, refs = refs[:HELD], refs[HELD : HELD + LATER], refs[HELD + LATER :]
     outs, refs = refs[:2], refs[2:]
-    copies = []
+    wso_ref, wti_ref, wto_ref = later
     if first:
-        later_hbm, later, refs = later, refs[:LATER], refs[LATER:]
-        wti_raw = refs[-2]
-        targets = (later[0], wti_raw, later[2])
-        copies = [pltpu.make_async_copy(*pair, refs[-1].at[i]) for i, pair in enumerate(zip(later_hbm, targets))]
-        start_all(copies)
-    cross_ref, mixed_ref, keys_ref, squares_ref = refs[:4]
-    wso_ref, wti_ref, wto_ref = later
+        wti_raw, wti_ref, refs = wti_ref, refs[0], refs[1:]
+    cross_ref, mixed_ref, keys_ref, squares_ref = refs
     (
         key_plan_ref,
         value_plan_ref,
@@ -360,9 +355,6 @@
             keys_ref[q] = keys.astype(bf16)
             if b == 0:
                 queries = next(steps, None) if q < 4 else queries
-        if b == blocks - 1:
-            for copy in copies:
-                copy.wait()
         for q in range(slots):
             if b == blocks - 1:
                 for to, source in turns[q :: slots]:
@@ -545,8 +537,10 @@
         head_sum,
         pos_frame,
         fresh_noise,
+        spatial_out,
+        temporal_turned,
+        temporal_out,
     ]
-    later = [spatial_out, temporal_turned, temporal_out]
     held = [
         pltpu.VMEM((token_blocks, slots, PLAN, WIDE), bf16),
         pltpu.VMEM((token_blocks, slots, LANES + FRAMES * PIECE, INNER), bf16),
@@ -576,6 +570,7 @@
         ],
         "slot_plan",
     )
+    held, later = held[:HELD], held[HELD:]
     result_shape = pltpu.VMEM((2, blocks * FRAMES, CH, tokens), f32)
     for step in range(STEPS):
         last = step == STEPS - 1
@@ -584,17 +579,16 @@
         scratch = [pltpu.VMEM((devices, lanes, LANES), f32), pltpu.VMEM((lanes, INNER), f32)]
         scratch += [pltpu.VMEM((slots, FRAMES * LANES, WIDE), bf16)] * 2
         if step == 0:
-            later_shapes = (spatial_out.shape, (D, 2 * WIDE + INNER), temporal_out.shape)
-            out_shape += [pltpu.VMEM(shape, bf16) for shape in later_shapes]
-            scratch += [pltpu.VMEM(temporal_turned.shape, bf16), dma((LATER,))]
-        lat, pieces, *brought = call(
+            out_shape += [pltpu.VMEM((D, 2 * WIDE + INNER), bf16)]
+        lat, pieces, *made = call(
             functools.partial(step_kernel, step=step),
             out_shape,
-            [(x, vmem) for x in (gathered, lat, *held)] + [(x, hbm if step == 0 else vmem) for x in later],
+            [(x, vmem) for x in (gathered, lat, *held, *later)],
             scratch,
             "denoise_step",
         )
-        later = brought or later
+        if made:
+            later = [later[0], *made, later[2]]
 
     received = lax.ppermute(pieces, "tm", partner)
     return tuple((lat[i] + received[i]).reshape(queue_latents.shape) for i in range(2))

time: 70.4 us -> 68.8 us (0.977)
  Pallas kernels: 32.2 us -> 30.7 us
    pallas_call x4, Pallas kernels: 32.2 us -> 30.7 us  [call(): pl.pallas_call(kernel, out_shape=out_shape, in_specs=[spec for _, spec in...]
where the time goes in v5:
time: 68.8 us; the launch traced here: 68.6 us
  blocking collectives  35.1 us (51%)
  Pallas kernels  30.7 us (45%)
  waiting for transfers between devices  1.33 us (2%)
    all_to_all x3, blocking collectives, per_device(): lax.all_to_all(pieces, axes, split_axis=0, concat_axis=0, tiled=True)  35.1 us
    pallas_call x4, Pallas kernels, call(): pl.pallas_call(kernel, out_shape=out_shape, in_specs=[spec for _, spec in...  30.7 us
  transfers between devices with their start and end apart: 1, of which 1 were waited for; matrix products, arithmetic and copies ran while one was open for 0% of the time, Pallas kernels for 0%

profile of v5, /device:TPU:0, one launch (start us, length us, event | category | flops | bytes accessed | tf_op | source)
XLA Modules:
  0.0 68.6 jit_solution(4461711711278797801)
XLA Ops:
  0.6 8.2 %slot_plan.1 = (bf16[1,8,160,640]{3,2,1,0:T(8,128)(2,1)S(1)}, bf16[1,8,192,576]{3,2,1,0:T(8,128)(2,1)S(1)}, f32[8,8,1152]{2,1,0:T(8,128)S(1)}, f32[8,640]{1,0:T(...) custom-call(s32[8]{0:T(128)} %levels_hbm.1, ...), custom_call_target="tpu_custom_call" | custom-call | tf_op jit(solution)/shard_map/slot_plan/pallas_call | solution.py:520
  8.8 15.1 %all_to_all.15.pieces_ref = bf16[16,32,128]{2,1,0:T(8,128)(2,1)S(1)} all-to-all(bf16[16,32,128]{2,1,0:T(8,128)(2,1)S(1)} %get-tuple-element.27), channel_id=1, replica_groups=mesh['clip'=2,'tm'=2,'space'=8] {'space','tm'}, dimensions={0} | all-to-all | bytes 262144 | tf_op jit(solution)/shard_map/all_to_all | solution.py:577
  23.9 8.0 %denoise_step.3 = (f32[16,128]{1,0:T(8,128)S(1)}, bf16[16,24,128]{2,1,0:T(8,128)(2,1)S(1)}, bf16[1152,1856]{1,0:T(8,128)(2,1)S(1)}) custom-call(bf16[16,32,128]{2,1,0:T(8,128)(2,1)S(1)} %all_to_all.15.pieces_ref, f32[16,128]{1,0:T(8,128)S(1)} %get-tuple-element.28.lat_ref, bf16[1,8,160,640]{3,2,1,0:T(8,128)(2,1)S(1)} %get-tuple-element.29.refs_0_, ...), custom_call_target="tpu_custom_call" | custom-call | tf_op jit(solution)/shard_map/denoise_step/pallas_call | solution.py:520
  31.9 10.0 %all_to_all.16.pieces_ref = bf16[16,24,128]{2,1,0:T(8,128)(2,1)S(1)} all-to-all(bf16[16,24,128]{2,1,0:T(8,128)(2,1)S(1)} %get-tuple-element.45), channel_id=1, replica_groups=mesh['clip'=2,'tm'=2,'space'=8] {'space','tm'}, dimensions={0} | all-to-all | bytes 196608 | tf_op jit(solution)/shard_map/all_to_all | solution.py:577
  41.9 7.5 %denoise_step.4 = (f32[16,128]{1,0:T(8,128)S(1)}, bf16[16,24,128]{2,1,0:T(8,128)(2,1)S(1)}) custom-call(bf16[16,24,128]{2,1,0:T(8,128)(2,1)S(1)} %all_to_all.16.pieces_ref, f32[16,128]{1,0:T(8,128)S(1)} %get-tuple-element.46.lat_ref, bf16[1,8,160,640]{3,2,1,0:T(8,128)(2,1)S(1)} %get-tuple-element.29.refs_0_, ...), custom_call_target="tpu_custom_call" | custom-call | tf_op jit(solution)/shard_map/denoise_step/pallas_call | solution.py:520
  49.4 10.0 %all_to_all.17.pieces_ref = bf16[16,24,128]{2,1,0:T(8,128)(2,1)S(1)} all-to-all(bf16[16,24,128]{2,1,0:T(8,128)(2,1)S(1)} %get-tuple-element.48), channel_id=1, replica_groups=mesh['clip'=2,'tm'=2,'space'=8] {'space','tm'}, dimensions={0} | all-to-all | bytes 196608 | tf_op jit(solution)/shard_map/all_to_all | solution.py:577
  59.4 7.1 %denoise_step.5 = (f32[2,8,16,16]{3,2,1,0:T(8,128)S(1)}, f32[2,8,16,16]{3,2,1,0:T(8,128)S(1)}) custom-call(bf16[16,24,128]{2,1,0:T(8,128)(2,1)S(1)} %all_to_all.17.pieces_ref, f32[16,128]{1,0:T(8,128)S(1)} %get-tuple-element.49.lat_ref, bf16[1,8,160,640]{3,2,1,0:T(8,128)(2,1)S(1)} %get-tuple-element.29.refs_0_, ...), custom_call_target="tpu_custom_call" | custom-call | tf_op jit(solution)/shard_map/denoise_step/pallas_call | solution.py:520
  66.5 0.1 collective-permute-start
  66.6 1.3 %collective-permute-done = f32[2,8,16,16]{3,2,1,0:T(8,128)S(1)} collective-permute-done((f32[2,8,16,16]{3,2,1,0:T(8,128)S(1)}, f32[2,8,16,16]{3,2,1,0:T(8,128)S(1)}, u32[]{:S(2)}, u32[]{:S(2)}) %collective-permute-start) | collective-permute-done | bytes 16416 | tf_op jit(solution)/shard_map/ppermute | solution.py:593
  67.9 0.7 slice_add_fusion
Async XLA Ops:
  66.5 1.4 %collective-permute-start = (f32[2,8,16,16]{3,2,1,0:T(8,128)S(1)}, f32[2,8,16,16]{3,2,1,0:T(8,128)S(1)}, u32[]{:S(2)}, u32[]{:S(2)}) collective-permute-start(f32[2,8,16,16]{3,2,1,0:T(8,128)S(1)} %get-tuple-element.51), channel_id=1, source_target_pairs={{0,8},{8,0},{1,9},{9,1},{2,10},{10,2},{3,11},{11,3},{4,12},{12,4},... | collective-permute-start | bytes 49160 | tf_op jit(solution)/shard_map/ppermute | solution.py:593

commit v6 on v5

--- a/solution.py
+++ b/solution.py
@@ -355,6 +355,7 @@
             keys_ref[q] = keys.astype(bf16)
             if b == 0:
                 queries = next(steps, None) if q < 4 else queries
+        products = {}
         for q in range(slots):
             if b == blocks - 1:
                 for to, source in turns[q :: slots]:
@@ -365,6 +366,9 @@
                 g = q * FRAMES + f
                 spread = (queries[g * own : (g + 1) * own][None] * masks).reshape(HEADS * own, WIDE).astype(bf16)
                 scores.append(dot_nt(keys_ref[q, at], spread))
+            products[q] = sums, scores
+        for q in range(slots):
+            sums, scores = products[q]
             scores = jnp.concatenate(scores, axis=1)
             weights[b, q] = jnp.exp(scores * lax.rsqrt(sums * (1.0 / HD) + epsilon))
             totals[q] = totals[q] + jnp.sum(weights[b, q], axis=0, keepdims=True)

time: 68.8 us -> 68.8 us (level)
  no operation moved by 1% of the time
where the time goes in v6:
time: 68.8 us; the launch traced here: 68.6 us
  blocking collectives  35.1 us (51%)
  Pallas kernels  30.7 us (45%)
  waiting for transfers between devices  1.33 us (2%)
    all_to_all x3, blocking collectives, per_device(): lax.all_to_all(pieces, axes, split_axis=0, concat_axis=0, tiled=True)  35.1 us
    pallas_call x4, Pallas kernels, call(): pl.pallas_call(kernel, out_shape=out_shape, in_specs=[spec for _, spec in...  30.7 us
  transfers between devices with their start and end apart: 1, of which 1 were waited for; matrix products, arithmetic and copies ran while one was open for 0% of the time, Pallas kernels for 0%

profile of v6, /device:TPU:0, one launch (start us, length us, event | category | flops | bytes accessed | tf_op | source)
XLA Modules:
  0.0 68.6 jit_solution(4461711711278797801)
XLA Ops:
  0.6 8.2 %slot_plan.1 = (bf16[1,8,160,640]{3,2,1,0:T(8,128)(2,1)S(1)}, bf16[1,8,192,576]{3,2,1,0:T(8,128)(2,1)S(1)}, f32[8,8,1152]{2,1,0:T(8,128)S(1)}, f32[8,640]{1,0:T(...) custom-call(s32[8]{0:T(128)} %levels_hbm.1, ...), custom_call_target="tpu_custom_call" | custom-call | tf_op jit(solution)/shard_map/slot_plan/pallas_call | solution.py:524
  8.8 15.1 %all_to_all.15.pieces_ref = bf16[16,32,128]{2,1,0:T(8,128)(2,1)S(1)} all-to-all(bf16[16,32,128]{2,1,0:T(8,128)(2,1)S(1)} %get-tuple-element.27), channel_id=1, replica_groups=mesh['clip'=2,'tm'=2,'space'=8] {'space','tm'}, dimensions={0} | all-to-all | bytes 262144 | tf_op jit(solution)/shard_map/all_to_all | solution.py:581
  23.9 8.0 %denoise_step.3 = (f32[16,128]{1,0:T(8,128)S(1)}, bf16[16,24,128]{2,1,0:T(8,128)(2,1)S(1)}, bf16[1152,1856]{1,0:T(8,128)(2,1)S(1)}) custom-call(bf16[16,32,128]{2,1,0:T(8,128)(2,1)S(1)} %all_to_all.15.pieces_ref, f32[16,128]{1,0:T(8,128)S(1)} %get-tuple-element.28.lat_ref, bf16[1,8,160,640]{3,2,1,0:T(8,128)(2,1)S(1)} %get-tuple-element.29.refs_0_, ...), custom_call_target="tpu_custom_call" | custom-call | tf_op jit(solution)/shard_map/denoise_step/pallas_call | solution.py:524
  31.9 10.0 %all_to_all.16.pieces_ref = bf16[16,24,128]{2,1,0:T(8,128)(2,1)S(1)} all-to-all(bf16[16,24,128]{2,1,0:T(8,128)(2,1)S(1)} %get-tuple-element.45), channel_id=1, replica_groups=mesh['clip'=2,'tm'=2,'space'=8] {'space','tm'}, dimensions={0} | all-to-all | bytes 196608 | tf_op jit(solution)/shard_map/all_to_all | solution.py:581
  41.9 7.5 %denoise_step.4 = (f32[16,128]{1,0:T(8,128)S(1)}, bf16[16,24,128]{2,1,0:T(8,128)(2,1)S(1)}) custom-call(bf16[16,24,128]{2,1,0:T(8,128)(2,1)S(1)} %all_to_all.16.pieces_ref, f32[16,128]{1,0:T(8,128)S(1)} %get-tuple-element.46.lat_ref, bf16[1,8,160,640]{3,2,1,0:T(8,128)(2,1)S(1)} %get-tuple-element.29.refs_0_, ...), custom_call_target="tpu_custom_call" | custom-call | tf_op jit(solution)/shard_map/denoise_step/pallas_call | solution.py:524
  49.4 10.0 %all_to_all.17.pieces_ref = bf16[16,24,128]{2,1,0:T(8,128)(2,1)S(1)} all-to-all(bf16[16,24,128]{2,1,0:T(8,128)(2,1)S(1)} %get-tuple-element.48), channel_id=1, replica_groups=mesh['clip'=2,'tm'=2,'space'=8] {'space','tm'}, dimensions={0} | all-to-all | bytes 196608 | tf_op jit(solution)/shard_map/all_to_all | solution.py:581
  59.4 7.1 %denoise_step.5 = (f32[2,8,16,16]{3,2,1,0:T(8,128)S(1)}, f32[2,8,16,16]{3,2,1,0:T(8,128)S(1)}) custom-call(bf16[16,24,128]{2,1,0:T(8,128)(2,1)S(1)} %all_to_all.17.pieces_ref, f32[16,128]{1,0:T(8,128)S(1)} %get-tuple-element.49.lat_ref, bf16[1,8,160,640]{3,2,1,0:T(8,128)(2,1)S(1)} %get-tuple-element.29.refs_0_, ...), custom_call_target="tpu_custom_call" | custom-call | tf_op jit(solution)/shard_map/denoise_step/pallas_call | solution.py:524
  66.5 0.1 collective-permute-start
  66.6 1.3 %collective-permute-done = f32[2,8,16,16]{3,2,1,0:T(8,128)S(1)} collective-permute-done((f32[2,8,16,16]{3,2,1,0:T(8,128)S(1)}, f32[2,8,16,16]{3,2,1,0:T(8,128)S(1)}, u32[]{:S(2)}, u32[]{:S(2)}) %collective-permute-start) | collective-permute-done | bytes 16416 | tf_op jit(solution)/shard_map/ppermute | solution.py:597
  67.9 0.7 slice_add_fusion
Async XLA Ops:
  66.5 1.4 %collective-permute-start = (f32[2,8,16,16]{3,2,1,0:T(8,128)S(1)}, f32[2,8,16,16]{3,2,1,0:T(8,128)S(1)}, u32[]{:S(2)}, u32[]{:S(2)}) collective-permute-start(f32[2,8,16,16]{3,2,1,0:T(8,128)S(1)} %get-tuple-element.51), channel_id=1, source_target_pairs={{0,8},{8,0},{1,9},{9,1},{2,10},{10,2},{3,11},{11,3},{4,12},{12,4},... | collective-permute-start | bytes 49160 | tf_op jit(solution)/shard_map/ppermute | solution.py:597

commit v7 on v6

--- a/solution.py
+++ b/solution.py
@@ -137,8 +137,8 @@
             left_ref[q * PLAN : (q + 1) * PLAN] = jnp.concatenate(
                 [pos * scale, embed * scale, shift_rows], axis=0
             ).astype(bf16)
-        for ref, weight in ((key_plan_ref, weight_ref[INNER : 2 * INNER]), (value_plan_ref, weight_ref[2 * INNER :])):
-            product = dot_nt(left_ref[...], weight)
+        products = [dot_nt(left_ref[...], weight_ref[i * INNER : (i + 1) * INNER]) for i in (1, 2)]
+        for ref, product in zip((key_plan_ref, value_plan_ref), products):
             for q in range(slots):
                 rows = product[q * PLAN : (q + 1) * PLAN]
                 group = rows[tokens:]

time: 68.8 us -> 68.8 us (level)
  no operation moved by 1% of the time
where the time goes in v7:
time: 68.8 us; the launch traced here: 68.6 us
  blocking collectives  35.1 us (51%)
  Pallas kernels  30.7 us (45%)
  waiting for transfers between devices  1.33 us (2%)
    all_to_all x3, blocking collectives, per_device(): lax.all_to_all(pieces, axes, split_axis=0, concat_axis=0, tiled=True)  35.1 us
    pallas_call x4, Pallas kernels, call(): pl.pallas_call(kernel, out_shape=out_shape, in_specs=[spec for _, spec in...  30.7 us
  transfers between devices with their start and end apart: 1, of which 1 were waited for; matrix products, arithmetic and copies ran while one was open for 0% of the time, Pallas kernels for 0%

profile of v7, /device:TPU:0, one launch (start us, length us, event | category | flops | bytes accessed | tf_op | source)
XLA Modules:
  0.0 68.6 jit_solution(10379277717095144472)
XLA Ops:
  0.6 8.1 %slot_plan.1 = (bf16[1,8,160,640]{3,2,1,0:T(8,128)(2,1)S(1)}, bf16[1,8,192,576]{3,2,1,0:T(8,128)(2,1)S(1)}, f32[8,8,1152]{2,1,0:T(8,128)S(1)}, f32[8,640]{1,0:T(...) custom-call(s32[8]{0:T(128)} %levels_hbm.1, ...), custom_call_target="tpu_custom_call" | custom-call | tf_op jit(solution)/shard_map/slot_plan/pallas_call | solution.py:524
  8.8 15.1 %all_to_all.15.pieces_ref = bf16[16,32,128]{2,1,0:T(8,128)(2,1)S(1)} all-to-all(bf16[16,32,128]{2,1,0:T(8,128)(2,1)S(1)} %get-tuple-element.27), channel_id=1, replica_groups=mesh['clip'=2,'tm'=2,'space'=8] {'space','tm'}, dimensions={0} | all-to-all | bytes 262144 | tf_op jit(solution)/shard_map/all_to_all | solution.py:581
  23.9 8.0 %denoise_step.3 = (f32[16,128]{1,0:T(8,128)S(1)}, bf16[16,24,128]{2,1,0:T(8,128)(2,1)S(1)}, bf16[1152,1856]{1,0:T(8,128)(2,1)S(1)}) custom-call(bf16[16,32,128]{2,1,0:T(8,128)(2,1)S(1)} %all_to_all.15.pieces_ref, f32[16,128]{1,0:T(8,128)S(1)} %get-tuple-element.28.lat_ref, bf16[1,8,160,640]{3,2,1,0:T(8,128)(2,1)S(1)} %get-tuple-element.29.refs_0_, ...), custom_call_target="tpu_custom_call" | custom-call | tf_op jit(solution)/shard_map/denoise_step/pallas_call | solution.py:524
  31.9 10.0 %all_to_all.16.pieces_ref = bf16[16,24,128]{2,1,0:T(8,128)(2,1)S(1)} all-to-all(bf16[16,24,128]{2,1,0:T(8,128)(2,1)S(1)} %get-tuple-element.45), channel_id=1, replica_groups=mesh['clip'=2,'tm'=2,'space'=8] {'space','tm'}, dimensions={0} | all-to-all | bytes 196608 | tf_op jit(solution)/shard_map/all_to_all | solution.py:581
  41.9 7.5 %denoise_step.4 = (f32[16,128]{1,0:T(8,128)S(1)}, bf16[16,24,128]{2,1,0:T(8,128)(2,1)S(1)}) custom-call(bf16[16,24,128]{2,1,0:T(8,128)(2,1)S(1)} %all_to_all.16.pieces_ref, f32[16,128]{1,0:T(8,128)S(1)} %get-tuple-element.46.lat_ref, bf16[1,8,160,640]{3,2,1,0:T(8,128)(2,1)S(1)} %get-tuple-element.29.refs_0_, ...), custom_call_target="tpu_custom_call" | custom-call | tf_op jit(solution)/shard_map/denoise_step/pallas_call | solution.py:524
  49.4 10.0 %all_to_all.17.pieces_ref = bf16[16,24,128]{2,1,0:T(8,128)(2,1)S(1)} all-to-all(bf16[16,24,128]{2,1,0:T(8,128)(2,1)S(1)} %get-tuple-element.48), channel_id=1, replica_groups=mesh['clip'=2,'tm'=2,'space'=8] {'space','tm'}, dimensions={0} | all-to-all | bytes 196608 | tf_op jit(solution)/shard_map/all_to_all | solution.py:581
  59.4 7.1 %denoise_step.5 = (f32[2,8,16,16]{3,2,1,0:T(8,128)S(1)}, f32[2,8,16,16]{3,2,1,0:T(8,128)S(1)}) custom-call(bf16[16,24,128]{2,1,0:T(8,128)(2,1)S(1)} %all_to_all.17.pieces_ref, f32[16,128]{1,0:T(8,128)S(1)} %get-tuple-element.49.lat_ref, bf16[1,8,160,640]{3,2,1,0:T(8,128)(2,1)S(1)} %get-tuple-element.29.refs_0_, ...), custom_call_target="tpu_custom_call" | custom-call | tf_op jit(solution)/shard_map/denoise_step/pallas_call | solution.py:524
  66.5 0.1 collective-permute-start
  66.6 1.3 %collective-permute-done = f32[2,8,16,16]{3,2,1,0:T(8,128)S(1)} collective-permute-done((f32[2,8,16,16]{3,2,1,0:T(8,128)S(1)}, f32[2,8,16,16]{3,2,1,0:T(8,128)S(1)}, u32[]{:S(2)}, u32[]{:S(2)}) %collective-permute-start) | collective-permute-done | bytes 16416 | tf_op jit(solution)/shard_map/ppermute | solution.py:597
  67.9 0.7 slice_add_fusion
Async XLA Ops:
  66.5 1.4 %collective-permute-start = (f32[2,8,16,16]{3,2,1,0:T(8,128)S(1)}, f32[2,8,16,16]{3,2,1,0:T(8,128)S(1)}, u32[]{:S(2)}, u32[]{:S(2)}) collective-permute-start(f32[2,8,16,16]{3,2,1,0:T(8,128)S(1)} %get-tuple-element.51), channel_id=1, source_target_pairs={{0,8},{8,0},{1,9},{9,1},{2,10},{10,2},{3,11},{11,3},{4,12},{12,4},... | collective-permute-start | bytes 49160 | tf_op jit(solution)/shard_map/ppermute | solution.py:597
